TPU v7x, 32 devices: a whole 2x2x4 slice. The times are simulated.
32 devices in a mesh: gx: 4 (over y, core), gy: 8 (over z, x).
Axes of the slice: x: 2, y: 2, z: 4, core: 2. Of those that a mesh axis runs over, the one named last changes fastest.
Arguments:
- interface_conditions: float32 [8, 512, 1024], P(None, 'gx', 'gy'), may hold values from -3 to 1.5, as said below
- level_warmth_profile: float32 [512, 5, 10, 1024], P(('gx', 'gy')), may hold values from -2 to -0.1
- class_coverage_share: float32 [512, 5, 1024], P(('gx', 'gy')), may hold values from 0.02 to 0.4
- class_floe_depth: float32 [512, 5, 1024], P(('gx', 'gy')), may hold values from 0.5 to 4
- class_drift_depth: float32 [512, 5, 1024], P(('gx', 'gy')), may hold values from 0.05 to 0.5
- floe_drift_speed: float32 [2, 512, 1024], P(None, 'gx', 'gy'), may hold values from -3 to 3
- internal_tension_tensor: float32 [3, 512, 1024], P(None, 'gx', 'gy'), may hold values from -3 to 3
- external_drive: float32 [4, 512, 1024], P(None, 'gx', 'gy'), may hold values from -2 to 2
- floe_weight: float32 [512, 1024], P('gx', 'gy'), may hold values from 0.3 to 3
- floe_pressure: float32 [512, 1024], P('gx', 'gy'), may hold values from 0.2 to 2
- holder_lookup: int32 [512, 1], P(('gx', 'gy')), may hold values from 0 to 7, as said below
- ground_tile_marker: int32 [512], P(('gx', 'gy')), may hold values from 0 to 1, as said below
Outputs:
- revised_level_warmth: float32 [512, 5, 10, 1024], P(('gx', 'gy'))
- interface_exchanges: float32 [8, 512, 1024], P(None, 'gx', 'gy')
- velocity_new: float32 [2, 512, 1024], P(None, 'gx', 'gy')
- stress_new: float32 [3, 512, 1024], P(None, 'gx', 'gy')
Inputs may be any that keep to these rules, and one draw needn't show every extreme that they name: `interface_conditions`: fields in order: ocean temperature in -0.2 to 0.1, salinity in 0.5 to 1, air temperature in -3 to -0.2, visible and near-infrared shortwave in 0 to 1, longwave in 0.5 to 1.5, snowfall and wind speed in 0 to 1. `holder_lookup`: each tile names one owner for at most 2 of its blocks. In every row of tiles there is one owner that every tile of the row names for exactly 2 blocks, none of them land. `ground_tile_marker`: 1 marks a land block.
All inputs are finite; a program needn't handle non-finite values.
Results may differ from a plain program's by a relative error of at most 0.0003.
Values sent between devices are 32-bit elements; how exact they have to be, the bound alone decides.
A program may use at most 128 MiB of HBM per device.

v0:
```python
import jax
import jax.numpy as jnp
from jax import lax
from jax.sharding import PartitionSpec as P

BS = 32
BPX = 4
BPY = 4
CAP = 2
FROZEN_LEVELS = 7
DRIFT_LEVELS = 3
POINT_QUANTITIES = 8
SUB = 4
TILE_POINTS = 1024
B = 16


RELAX_RATE = 0.5
ECC_SQUARED = 4.0
DELTA_FLOOR = 0.04
MOTION_STEP = 0.5
WATER_DRAG = 1.0
CORIOLIS = 0.3
HEAT_STEP = 0.5
SNOW_COND = 0.3
SNOW_GAIN = 0.3
GROWTH_RATE = 0.05


def padded(array, sides, width):
    for axis, dim in sides:
        peers, length = (lax.axis_size(axis), array.shape[dim])
        up = [(i, (i + 1) % peers) for i in range(peers - 1)]
        down = [(j, i) for i, j in up]
        last = lax.slice_in_dim(array, length - width, length, axis=dim)
        leading = lax.slice_in_dim(array, 0, width, axis=dim)
        before = lax.ppermute(last, axis, up)
        after = lax.ppermute(leading, axis, down)
        array = jnp.concatenate([before, array, after], axis=dim)
    return array


def column_step(layer_temp, cat_area, cat_thick, cat_snow, forcing_fields):
    ocean_temp = forcing_fields[:, 0:1]
    salinity = forcing_fields[:, 1:2]
    air_temp = forcing_fields[:, 2:3]
    visible = forcing_fields[:, 3:4]
    near_red = forcing_fields[:, 4:5]
    longwave = forcing_fields[:, 5:6]
    snowfall = forcing_fields[:, 6:7]
    wind_speed = forcing_fields[:, 7:8]
    snow_depth = cat_snow + SNOW_GAIN * snowfall
    layer_total = DRIFT_LEVELS + FROZEN_LEVELS
    depths = []
    heat_caps = []
    resist = []
    for layer_num in range(layer_total):
        old_temp = layer_temp[:, :, layer_num]
        if layer_num < DRIFT_LEVELS:
            layer_depth = snow_depth / DRIFT_LEVELS
            heat_cap = jnp.ones_like(layer_depth)
            conduct = SNOW_COND
        else:
            brine_term = salinity * (0.2 + 0.1 * (layer_num - DRIFT_LEVELS))
            layer_depth = cat_thick / FROZEN_LEVELS
            heat_cap = 1.0 + 0.2 * brine_term / (old_temp * old_temp + 0.1)
            conduct = 2.0 + 0.1 * brine_term / (old_temp - 0.5)
        depths.append(layer_depth)
        heat_caps.append(heat_cap)
        resist.append(layer_depth / conduct)
    top_cond = 1.0 / (0.5 * resist[0] + 1.0 / (1.0 + 2.0 * wind_speed))
    bottom_cond = 2.0 / resist[-1]
    inner_cond = [
        1.0 / (0.5 * (resist[layer_num] + resist[layer_num + 1]))
        for layer_num in range(layer_total - 1)
    ]
    cond_above = [top_cond] + inner_cond
    cond_below = inner_cond + [bottom_cond]
    sweep_ratio = []
    sweep_value = []
    for layer_num in range(layer_total):
        mass_term = heat_caps[layer_num] * depths[layer_num] / HEAT_STEP
        diagonal = mass_term + cond_above[layer_num] + cond_below[layer_num]
        source = mass_term * layer_temp[:, :, layer_num]
        if layer_num == 0:
            source = (
                source + top_cond * air_temp + 0.25 * visible + 0.45 * near_red + 0.3 * longwave
            )
        if layer_num == layer_total - 1:
            source = source + bottom_cond * ocean_temp
        if layer_num > 0:
            pivot_term = diagonal - cond_above[layer_num] * sweep_ratio[-1]
            carried = source + cond_above[layer_num] * sweep_value[-1]
        else:
            pivot_term = diagonal
            carried = source
        sweep_ratio.append(cond_below[layer_num] / pivot_term)
        sweep_value.append(carried / pivot_term)
    solved = [sweep_value[-1]]
    for layer_num in range(layer_total - 2, -1, -1):
        solved.insert(0, sweep_value[layer_num] + sweep_ratio[layer_num] * solved[0])
    advanced_warmth = jnp.stack(solved, axis=2)
    bottom_flux = bottom_cond * (solved[-1] - ocean_temp)
    growth = -GROWTH_RATE * bottom_flux
    energy = heat_caps[0] * depths[0] * solved[0]
    for layer_num in range(1, layer_total):
        energy = energy + heat_caps[layer_num] * depths[layer_num] * solved[layer_num]
    light_through = 0.7 * visible * jnp.exp(-5.0 * snow_depth - 1.5 * cat_thick)
    flux_terms = [
        bottom_flux,
        top_cond * (air_temp - solved[0]),
        light_through,
        solved[0],
        snow_depth,
        cat_thick + growth,
        0.1 * energy,
        growth * salinity,
    ]
    slot_fluxes = jnp.stack(
        [jnp.sum(cat_area * term_value, axis=1) for term_value in flux_terms], axis=1
    )
    return (advanced_warmth, slot_fluxes)


def strain_rates(drift_kinematics):
    east_vel = drift_kinematics[0]
    north_vel = drift_kinematics[1]
    du_x = 0.5 * (east_vel[2:, 1:-1] - east_vel[:-2, 1:-1])
    du_y = 0.5 * (east_vel[1:-1, 2:] - east_vel[1:-1, :-2])
    dv_x = 0.5 * (north_vel[2:, 1:-1] - north_vel[:-2, 1:-1])
    dv_y = 0.5 * (north_vel[1:-1, 2:] - north_vel[1:-1, :-2])
    return (du_x + dv_y, du_x - dv_y, du_y + dv_x)


def update_stress(stress_old, strength, drift_kinematics):
    diverge, tension, shearing = strain_rates(drift_kinematics)
    spread = jnp.sqrt(
        diverge * diverge + (tension * tension + shearing * shearing) / ECC_SQUARED + DELTA_FLOOR
    )
    ratio = strength / spread
    first = (stress_old[0] + RELAX_RATE * ratio * (diverge - spread)) / (1.0 + RELAX_RATE)
    second = (stress_old[1] + RELAX_RATE * ratio * tension / ECC_SQUARED) / (1.0 + RELAX_RATE)
    third = (stress_old[2] + RELAX_RATE * ratio * shearing / (2.0 * ECC_SQUARED)) / (
        1.0 + RELAX_RATE
    )
    return jnp.stack([first, second, third])


def stress_force(stress_pad):
    stress_sum = stress_pad[0] + stress_pad[1]
    differ = stress_pad[0] - stress_pad[1]
    shear_part = stress_pad[2]
    force_x = 0.25 * (stress_sum[2:, 1:-1] - stress_sum[:-2, 1:-1]) + 0.5 * (
        shear_part[1:-1, 2:] - shear_part[1:-1, :-2]
    )
    force_y = 0.25 * (differ[1:-1, 2:] - differ[1:-1, :-2]) + 0.5 * (
        shear_part[2:, 1:-1] - shear_part[:-2, 1:-1]
    )
    return (force_x, force_y)


def update_motion(drift_kinematics, force_x, force_y, floe_weight, external_drive, water_mask):
    east_vel = drift_kinematics[0]
    north_vel = drift_kinematics[1]
    denominator = floe_weight + MOTION_STEP * WATER_DRAG
    new_east = (
        floe_weight * east_vel
        + MOTION_STEP
        * (
            force_x
            + external_drive[0]
            + WATER_DRAG * external_drive[2]
            + CORIOLIS * floe_weight * north_vel
        )
    ) / denominator
    new_north = (
        floe_weight * north_vel
        + MOTION_STEP
        * (
            force_y
            + external_drive[1]
            + WATER_DRAG * external_drive[3]
            - CORIOLIS * floe_weight * east_vel
        )
    ) / denominator
    return jnp.stack([new_east * water_mask, new_north * water_mask])


def to_blocks(tile_data):
    field_count, row_count, column_count = tile_data.shape
    shaped = tile_data.reshape(field_count, BPX, BS, BPY, BS)
    return shaped.transpose(1, 3, 0, 2, 4).reshape(B, field_count, TILE_POINTS)


def from_blocks(block_data):
    field_count = block_data.shape[1]
    shaped = block_data.reshape(BPX, BPY, field_count, BS, BS)
    return shaped.transpose(2, 0, 3, 1, 4).reshape(field_count, BPX * BS, BPY * BS)


def slot_rank(target, slot_covered):
    length = target.shape[0]
    earlier = lax.broadcasted_iota(jnp.int32, (length, length), 1) < lax.broadcasted_iota(
        jnp.int32, (length, length), 0
    )
    matching = (target[:, None] == target[None, :]) & (slot_covered[None, :] == 1) & earlier
    return jnp.sum(matching.astype(jnp.int32), axis=1)


def local(
    interface_conditions,
    level_warmth_profile,
    class_coverage_share,
    class_floe_depth,
    class_drift_depth,
    floe_drift_speed,
    internal_tension_tensor,
    external_drive,
    floe_weight,
    floe_pressure,
    holder_lookup,
    ground_tile_marker,
):
    group_size = lax.axis_size("gy")
    slot_count = group_size * CAP
    blocks_of_grid = to_blocks(interface_conditions)
    target = holder_lookup[:, 0]
    slot_covered = 1 - ground_tile_marker
    order_rank = slot_rank(target, slot_covered)
    own_slot = target * CAP + order_rank
    slot_iota = lax.broadcasted_iota(jnp.int32, (B, slot_count), 1)
    own_choose = ((own_slot[:, None] == slot_iota) & (slot_covered[:, None] == 1)).astype(
        jnp.float32
    )
    outgoing = jnp.einsum(
        "bs,bfc->sfc", own_choose, blocks_of_grid, precision=lax.Precision.HIGHEST
    )
    flags = jnp.sum(own_choose, axis=0)
    parcel, occupied_mask = (
        lax.all_to_all(
            outgoing.reshape(group_size, CAP, POINT_QUANTITIES, TILE_POINTS),
            "gy",
            split_axis=0,
            concat_axis=0,
            tiled=True,
        ),
        lax.all_to_all(
            flags.reshape(group_size, CAP), "gy", split_axis=0, concat_axis=0, tiled=True
        ),
    )
    parcel = parcel.reshape(slot_count, POINT_QUANTITIES, TILE_POINTS)
    occupied_mask = occupied_mask.reshape(slot_count)
    advanced_warmth, slot_fluxes = column_step(
        level_warmth_profile, class_coverage_share, class_floe_depth, class_drift_depth, parcel
    )
    revised_level_warmth = jnp.where(
        occupied_mask[:, None, None, None] > 0.5, advanced_warmth, level_warmth_profile
    )
    returned = lax.all_to_all(
        slot_fluxes.reshape(group_size, CAP, 8, TILE_POINTS),
        "gy",
        split_axis=0,
        concat_axis=0,
        tiled=True,
    )
    returned = returned.reshape(slot_count, 8, TILE_POINTS)
    block_fluxes = jnp.einsum("bs,sfc->bfc", own_choose, returned, precision=lax.Precision.HIGHEST)
    interface_exchanges = from_blocks(block_fluxes)
    land_tile = (1.0 - ground_tile_marker.astype(jnp.float32)).reshape(BPX, BPY)
    water_mask = jnp.repeat(jnp.repeat(land_tile, BS, axis=0), BS, axis=1)
    drift_kinematics = floe_drift_speed
    tension_components = internal_tension_tensor
    strength_pad = padded(floe_pressure, (("gx", 0), ("gy", 1)), 1)
    for subcycle in range(SUB):
        extended = padded(
            jnp.concatenate([drift_kinematics, tension_components], axis=0),
            (("gx", 1), ("gy", 2)),
            2,
        )
        wide_stress = update_stress(extended[2:5, 1:-1, 1:-1], strength_pad, extended[0:2])
        force_x, force_y = stress_force(wide_stress)
        drift_kinematics = update_motion(
            drift_kinematics, force_x, force_y, floe_weight, external_drive, water_mask
        )
        tension_components = wide_stress[:, 1:-1, 1:-1]
    return (revised_level_warmth, interface_exchanges, drift_kinematics, tension_components)


def solution(mesh):
    return jax.shard_map(
        local,
        mesh=mesh,
        in_specs=(
            P(None, "gx", "gy"),
            P(("gx", "gy"), None, None, None),
            P(("gx", "gy"), None, None),
            P(("gx", "gy"), None, None),
            P(("gx", "gy"), None, None),
            P(None, "gx", "gy"),
            P(None, "gx", "gy"),
            P(None, "gx", "gy"),
            P("gx", "gy"),
            P("gx", "gy"),
            P(("gx", "gy"), None),
            P(("gx", "gy")),
        ),
        out_specs=(
            P(("gx", "gy"), None, None, None),
            P(None, "gx", "gy"),
            P(None, "gx", "gy"),
            P(None, "gx", "gy"),
        ),
        check_vma=False,
    )
```

profile of v0, /device:TPU:0, one launch (start us, length us, event | category | flops | bytes accessed | tf_op | source)
XLA Modules:
  0.0 174.3 jit_solution(8053922851466837595)
XLA Ops:
  4.2 3.1 %collective-permute-start = (f32[5,2,128]{1,2,0:T(8,128)S(1)}, f32[5,2,128]{1,2,0:T(8,128)S(1)}, u32[]{:S(2)}, u32[]{:S(2)}) collective-permute-start(f32[5,2,128]{1,2,0:T(8,128)S(1)} %get-tuple-element.128), channel_id=1, source_target_pairs={{0,8},{8,16},{16,24},{1,9},{9,17},{17,25},{2,10},{10,18},{18,26},{... | collective-permute-start | bytes 15368 | tf_op jit(solution)/shard_map/ppermute | solution.py:37
  9.4 5.1 %collective-permute-start.4 = (f32[1,128]{0,1:T(8,128)S(1)}, f32[1,128]{0,1:T(8,128)S(1)}, u32[]{:S(2)}, u32[]{:S(2)}) collective-permute-start(f32[1,128]{0,1:T(8,128)S(1)} %copy.211), channel_id=1, source_target_pairs={{0,8},{8,16},{16,24},{1,9},{9,17},{17,25},{2,10},{10,18},{18,26},{... | collective-permute-start | bytes 1544 | tf_op jit(solution)/shard_map/ppermute | solution.py:37
  20.9 4.5 %collective-permute-start.2 = (f32[5,132,2]{1,2,0:T(2,128)S(1)}, f32[5,132,2]{1,2,0:T(2,128)S(1)}, u32[]{:S(2)}, u32[]{:S(2)}) collective-permute-start(f32[5,132,2]{1,2,0:T(2,128)S(1)} %get-tuple-element.85), channel_id=1, source_target_pairs={{0,1},{1,2},{2,3},{3,4},{4,5},{5,6},{6,7},{8,9},{9,10},{10,11},{11... | collective-permute-start | bytes 15848 | tf_op jit(solution)/shard_map/ppermute | solution.py:37
  26.8 4.9 %collective-permute-start.6 = (f32[130,1]{0,1:T(1,128)S(1)}, f32[130,1]{0,1:T(1,128)S(1)}, u32[]{:S(2)}, u32[]{:S(2)}) collective-permute-start(f32[130,1]{0,1:T(1,128)S(1)} %get-tuple-element.134), channel_id=1, source_target_pairs={{0,1},{1,2},{2,3},{3,4},{4,5},{5,6},{6,7},{8,9},{9,10},{10,11},{11... | collective-permute-start | bytes 1568 | tf_op jit(solution)/shard_map/ppermute | solution.py:37
  35.5 3.1 %collective-permute-start.8 = (f32[5,2,128]{1,2,0:T(8,128)S(1)}, f32[5,2,128]{1,2,0:T(8,128)S(1)}, u32[]{:S(2)}, u32[]{:S(2)}) collective-permute-start(f32[5,2,128]{1,2,0:T(8,128)S(1)} %get-tuple-element.126), channel_id=1, source_target_pairs={{0,8},{8,16},{16,24},{1,9},{9,17},{17,25},{2,10},{10,18},{18,26},{... | collective-permute-start | bytes 15368 | tf_op jit(solution)/shard_map/ppermute | solution.py:37
  41.1 5.4 %collective-permute-start.10 = (f32[5,132,2]{1,2,0:T(2,128)S(1)}, f32[5,132,2]{1,2,0:T(2,128)S(1)}, u32[]{:S(2)}, u32[]{:S(2)}) collective-permute-start(f32[5,132,2]{1,2,0:T(2,128)S(1)} %get-tuple-element.83), channel_id=1, source_target_pairs={{0,1},{1,2},{2,3},{3,4},{4,5},{5,6},{6,7},{8,9},{9,10},{10,11},{11... | collective-permute-start | bytes 15848 | tf_op jit(solution)/shard_map/ppermute | solution.py:37
  50.7 5.7 %collective-permute-start.12 = (f32[5,2,128]{1,2,0:T(8,128)S(1)}, f32[5,2,128]{1,2,0:T(8,128)S(1)}, u32[]{:S(2)}, u32[]{:S(2)}) collective-permute-start(f32[5,2,128]{1,2,0:T(8,128)S(1)} %get-tuple-element.124), channel_id=1, source_target_pairs={{0,8},{8,16},{16,24},{1,9},{9,17},{17,25},{2,10},{10,18},{18,26},{... | collective-permute-start | bytes 15368 | tf_op jit(solution)/shard_map/ppermute | solution.py:37
  57.3 8.1 %all-to-all-start = ((f32[8,1,2]{2,1,0:T(1,128)}), f32[8,1,2]{2,1,0:T(1,128)S(1)}, u32[]{:S(2)}, u32[]{:S(2)}) async-start(f32[8,1,2]{2,1,0:T(1,128)} %bitcast.3), calls=%async_computation | async-start | bytes 8192 | tf_op jit(solution)/shard_map/all_to_all | solution.py:247
  66.8 4.5 %collective-permute-start.14 = (f32[5,132,2]{1,2,0:T(2,128)S(1)}, f32[5,132,2]{1,2,0:T(2,128)S(1)}, u32[]{:S(2)}, u32[]{:S(2)}) collective-permute-start(f32[5,132,2]{1,2,0:T(2,128)S(1)} %get-tuple-element.81), channel_id=1, source_target_pairs={{0,1},{1,2},{2,3},{3,4},{4,5},{5,6},{6,7},{8,9},{9,10},{10,11},{11... | collective-permute-start | bytes 15848 | tf_op jit(solution)/shard_map/ppermute | solution.py:37
  71.4 2.2 %reshape.127 = f32[8,4,32,4,32]{4,3,2,1,0:T(4,128)} reshape(f32[8,128,128]{2,1,0:T(8,128)S(1)} %copy-done.18) | data formatting | bytes 1048576 | tf_op jit(solution)/shard_map/reshape | solution.py:191
  73.7 1.8 %copy.182 = f32[4,4,8,32,32]{4,3,1,0,2:T(8,128)S(1)} copy(f32[4,4,8,32,32]{4,1,3,0,2:T(4,128)} %bitcast.568) | data formatting | bytes 1048576 | tf_op jit(solution)/shard_map/transpose | solution.py:192
  80.4 5.6 %collective-permute-start.16 = (f32[5,2,128]{1,2,0:T(8,128)S(1)}, f32[5,2,128]{1,2,0:T(8,128)S(1)}, u32[]{:S(2)}, u32[]{:S(2)}) collective-permute-start(f32[5,2,128]{1,2,0:T(8,128)S(1)} %get-tuple-element.122), channel_id=1, source_target_pairs={{0,8},{8,16},{16,24},{1,9},{9,17},{17,25},{2,10},{10,18},{18,26},{... | collective-permute-start | bytes 15368 | tf_op jit(solution)/shard_map/ppermute | solution.py:37
  89.6 5.2 %collective-permute-start.18 = (f32[5,132,2]{1,2,0:T(2,128)S(1)}, f32[5,132,2]{1,2,0:T(2,128)S(1)}, u32[]{:S(2)}, u32[]{:S(2)}) collective-permute-start(f32[5,132,2]{1,2,0:T(2,128)S(1)} %get-tuple-element.79), channel_id=1, source_target_pairs={{0,1},{1,2},{2,3},{3,4},{4,5},{5,6},{6,7},{8,9},{9,10},{10,11},{11... | collective-permute-start | bytes 15848 | tf_op jit(solution)/shard_map/ppermute | solution.py:37
  94.8 6.0 %all-to-all-start.1 = ((f32[8,2,8,1024]{3,2,1,0:T(8,128)}), f32[8,2,8,1024]{3,2,1,0:T(8,128)}, u32[]{:S(2)}, u32[]{:S(2)}) async-start(f32[8,2,8,1024]{3,2,1,0:T(8,128)} %copy.183), calls=%async_computation.1 | async-start | bytes 1048576 | tf_op jit(solution)/shard_map/all_to_all | solution.py:240
  106.7 1.8 %pad_maximum_fusion.8 = f32[3,128,128]{1,2,0:T(8,128)} fusion(f32[1,130,130]{1,2,0:T(8,128)S(1)} %bitcast.569, f32[1,130,130]{1,2,0:T(8,128)} %bitcast.592, f32[1,130,130]{1,2,0:T(8,128)} %bitcast.593), kind=kLoop, calls=%fused_computation.183 | loop fusion | flops 98304 | bytes 399408 | tf_op jit(solution)/shard_map/stack | solution.py:146
  108.4 1.7 copy.230
  110.2 4.9 %all-to-all-done.1 = f32[8,2,8,1024]{3,2,1,0:T(8,128)} async-done(((f32[8,2,8,1024]{3,2,1,0:T(8,128)}), f32[8,2,8,1024]{3,2,1,0:T(8,128)}, u32[]{:S(2)}, u32[]{:S(2)}) %all-to-all-start.1) | async-done | bytes 524320 | tf_op jit(solution)/shard_map/all_to_all | solution.py:240
  115.1 4.0 %broadcast_multiply_fusion.1 = (f32[16,1,1024]{2,1,0:T(1,128)S(1)}, f32[16,1,1024]{2,1,0:T(1,128)S(1)}, f32[16,1,1024]{2,1,0:T(1,128)S(1)}, f32[16,1,1024]{2,1,0...) fusion(f32[16,8,1024]{2,1,0:T(8,128)} %bitcast.7), kind=kLoop, calls=%fused_computation.413 | loop fusion | flops 311296 | bytes 1703936 | tf_op jit(solution)/shard_map/mul | solution.py:117
  120.6 1.9 %multiply_divide_fusion.2 = (f32[16,5,1024]{2,0,1:T(8,128)S(1)}, f32[16,5,1024]{2,0,1:T(8,128)S(1)}, f32[16,5,1024]{2,0,1:T(8,128)S(1)}, f32[16,5,1024]{2,0,1:T(...) fusion(f32[16,5,10,1024]{3,0,2,1:T(8,128)S(1)} %copy-done, ...), kind=kLoop, calls=%fused_computation.151 | loop fusion | flops 10403840 | bytes 8257536 | tf_op jit(solution)/shard_map/div | solution.py:97
  123.8 2.7 %fusion.86 = (f32[16,1024]{1,0:T(8,128)S(1)}, f32[16,5,1024]{2,0,1:T(8,128)S(1)}, f32[16,5,1024]{2,0,1:T(8,128)S(1)}, f32[16,5,1024]{2,0,1:T(8,128)}, f32[16,5,1...) fusion(f32[16,5,1024]{2,0,1:T(8,128)S(1)} %copy-done.13, ...), kind=kLoop, calls=%fused_computation.129 | loop fusion | flops 9977856 | bytes 11927552 | tf_op jit(solution)/shard_map/reduce_sum | solution.py:120
  147.1 5.1 %all-to-all-start.2 = ((f32[8,2,8,1024]{3,1,2,0:T(2,128)}), f32[8,2,8,1024]{3,1,2,0:T(2,128)}, u32[]{:S(2)}, u32[]{:S(2)}) async-start(f32[8,2,8,1024]{3,1,2,0:T(2,128)} %constant_dynamic-update-slice_fusion), calls=%async_computation.2 | async-start | bytes 1048576 | tf_op jit(solution)/shard_map/all_to_all | solution.py:259
  152.2 1.8 %bitcast_dynamic-update-slice_fusion.5 = f32[16,5,10,1024]{3,0,2,1:T(8,128)} fusion(f32[16,5,10,1024]{3,0,2,1:T(8,128)} %bitcast_dynamic-update-slice_fusion.6, f32[16,5,1024]{2,0,1:T(8,128)} %get-tuple-element.50), kind=kLoop, calls=%fused_computation.115 | loop fusion | bytes 655360
  162.4 4.4 %broadcast_select_fusion = f32[16,5,10,1024]{3,0,2,1:T(8,128)} fusion(f32[16,5,10,1024]{3,0,2,1:T(8,128)} %bitcast_dynamic-update-slice_fusion.9, f32[16,5,10,1024]{3,0,2,1:T(8,128)S(1)} %copy-done, pred[16]{0:T(512)(128)(4,1)S(1)} %copy-done.21), kind=kLoop, calls=%fused_computation.3 | loop fusion | flops 819200 | bytes 9830416 | tf_op jit(solution)/shard_map/jit(_where)/select_n | solution.py:256
  169.7 2.8 %fusion.3 = f32[8,4,32,4,32]{4,3,2,0,1:T(4,128)S(1)} fusion(f32[8,32,32,16]{2,1,0,3:T(8,128)S(1)} %reshape.140, s32[4,4]{1,0:T(4,128)S(1)} %eq.71, pred[4,4]{1,0:T(4,128)(4,1)S(1)} %copy-done.20), kind=kOutput, calls=%fused_computation.4 | convolution fusion | flops 25166336 | bytes 1048656 | tf_op jit(solution)/shard_map/bs,sfc->bfc/dot_general | solution.py:267
  (189 shorter events, 76.3 us)
Async XLA Ops:
  2.9 16.6 %collective-permute-start.1 = (f32[5,2,128]{1,2,0:T(8,128)S(1)}, f32[5,2,128]{1,2,0:T(8,128)S(1)}, u32[]{:S(2)}, u32[]{:S(2)}) collective-permute-start(f32[5,2,128]{1,2,0:T(8,128)S(1)} %get-tuple-element.129), channel_id=1, source_target_pairs={{8,0},{16,8},{24,16},{9,1},{17,9},{25,17},{10,2},{18,10},{26,18},{... | collective-permute-start | bytes 15368 | tf_op jit(solution)/shard_map/ppermute | solution.py:38
  4.2 15.3 %collective-permute-start = (f32[5,2,128]{1,2,0:T(8,128)S(1)}, f32[5,2,128]{1,2,0:T(8,128)S(1)}, u32[]{:S(2)}, u32[]{:S(2)}) collective-permute-start(f32[5,2,128]{1,2,0:T(8,128)S(1)} %get-tuple-element.128), channel_id=1, source_target_pairs={{0,8},{8,16},{16,24},{1,9},{9,17},{17,25},{2,10},{10,18},{18,26},{... | collective-permute-start | bytes 15368 | tf_op jit(solution)/shard_map/ppermute | solution.py:37
  8.0 17.4 %collective-permute-start.5 = (f32[1,128]{0,1:T(8,128)S(1)}, f32[1,128]{0,1:T(8,128)S(1)}, u32[]{:S(2)}, u32[]{:S(2)}) collective-permute-start(f32[1,128]{0,1:T(8,128)S(1)} %copy.212), channel_id=1, source_target_pairs={{8,0},{16,8},{24,16},{9,1},{17,9},{25,17},{10,2},{18,10},{26,18},{... | collective-permute-start | bytes 1544 | tf_op jit(solution)/shard_map/ppermute | solution.py:38
  9.4 16.0 %collective-permute-start.4 = (f32[1,128]{0,1:T(8,128)S(1)}, f32[1,128]{0,1:T(8,128)S(1)}, u32[]{:S(2)}, u32[]{:S(2)}) collective-permute-start(f32[1,128]{0,1:T(8,128)S(1)} %copy.211), channel_id=1, source_target_pairs={{0,8},{8,16},{16,24},{1,9},{9,17},{17,25},{2,10},{10,18},{18,26},{... | collective-permute-start | bytes 1544 | tf_op jit(solution)/shard_map/ppermute | solution.py:37
  18.9 59.6 %copy-start.5 = (f32[128,128]{0,1:T(8,128)}, f32[128,128]{0,1:T(8,128)S(1)}, u32[]{:S(2)}) copy-start(f32[128,128]{0,1:T(8,128)S(1)} %copy.226) | copy-start | bytes 196612
  19.6 12.2 %collective-permute-start.3 = (f32[5,132,2]{1,2,0:T(2,128)S(1)}, f32[5,132,2]{1,2,0:T(2,128)S(1)}, u32[]{:S(2)}, u32[]{:S(2)}) collective-permute-start(f32[5,132,2]{1,2,0:T(2,128)S(1)} %get-tuple-element.86), channel_id=1, source_target_pairs={{1,0},{2,1},{3,2},{4,3},{5,4},{6,5},{7,6},{9,8},{10,9},{11,10},{12... | collective-permute-start | bytes 15848 | tf_op jit(solution)/shard_map/ppermute | solution.py:38
  20.9 10.9 %collective-permute-start.2 = (f32[5,132,2]{1,2,0:T(2,128)S(1)}, f32[5,132,2]{1,2,0:T(2,128)S(1)}, u32[]{:S(2)}, u32[]{:S(2)}) collective-permute-start(f32[5,132,2]{1,2,0:T(2,128)S(1)} %get-tuple-element.85), channel_id=1, source_target_pairs={{0,1},{1,2},{2,3},{3,4},{4,5},{5,6},{6,7},{8,9},{9,10},{10,11},{11... | collective-permute-start | bytes 15848 | tf_op jit(solution)/shard_map/ppermute | solution.py:37
  25.6 6.6 %collective-permute-start.7 = (f32[130,1]{0,1:T(1,128)S(1)}, f32[130,1]{0,1:T(1,128)S(1)}, u32[]{:S(2)}, u32[]{:S(2)}) collective-permute-start(f32[130,1]{0,1:T(1,128)S(1)} %get-tuple-element.135), channel_id=1, source_target_pairs={{1,0},{2,1},{3,2},{4,3},{5,4},{6,5},{7,6},{9,8},{10,9},{11,10},{12... | collective-permute-start | bytes 1568 | tf_op jit(solution)/shard_map/ppermute | solution.py:38
  26.8 6.2 %collective-permute-start.6 = (f32[130,1]{0,1:T(1,128)S(1)}, f32[130,1]{0,1:T(1,128)S(1)}, u32[]{:S(2)}, u32[]{:S(2)}) collective-permute-start(f32[130,1]{0,1:T(1,128)S(1)} %get-tuple-element.134), channel_id=1, source_target_pairs={{0,1},{1,2},{2,3},{3,4},{4,5},{5,6},{6,7},{8,9},{9,10},{10,11},{11... | collective-permute-start | bytes 1568 | tf_op jit(solution)/shard_map/ppermute | solution.py:37
  34.2 4.6 %collective-permute-start.9 = (f32[5,2,128]{1,2,0:T(8,128)S(1)}, f32[5,2,128]{1,2,0:T(8,128)S(1)}, u32[]{:S(2)}, u32[]{:S(2)}) collective-permute-start(f32[5,2,128]{1,2,0:T(8,128)S(1)} %get-tuple-element.127), channel_id=1, source_target_pairs={{8,0},{16,8},{24,16},{9,1},{17,9},{25,17},{10,2},{18,10},{26,18},{... | collective-permute-start | bytes 15368 | tf_op jit(solution)/shard_map/ppermute | solution.py:38
  35.5 4.3 %collective-permute-start.8 = (f32[5,2,128]{1,2,0:T(8,128)S(1)}, f32[5,2,128]{1,2,0:T(8,128)S(1)}, u32[]{:S(2)}, u32[]{:S(2)}) collective-permute-start(f32[5,2,128]{1,2,0:T(8,128)S(1)} %get-tuple-element.126), channel_id=1, source_target_pairs={{0,8},{8,16},{16,24},{1,9},{9,17},{17,25},{2,10},{10,18},{18,26},{... | collective-permute-start | bytes 15368 | tf_op jit(solution)/shard_map/ppermute | solution.py:37
  39.8 6.8 %collective-permute-start.11 = (f32[5,132,2]{1,2,0:T(2,128)S(1)}, f32[5,132,2]{1,2,0:T(2,128)S(1)}, u32[]{:S(2)}, u32[]{:S(2)}) collective-permute-start(f32[5,132,2]{1,2,0:T(2,128)S(1)} %get-tuple-element.84), channel_id=1, source_target_pairs={{1,0},{2,1},{3,2},{4,3},{5,4},{6,5},{7,6},{9,8},{10,9},{11,10},{12... | collective-permute-start | bytes 15848 | tf_op jit(solution)/shard_map/ppermute | solution.py:38
  41.1 6.8 %collective-permute-start.10 = (f32[5,132,2]{1,2,0:T(2,128)S(1)}, f32[5,132,2]{1,2,0:T(2,128)S(1)}, u32[]{:S(2)}, u32[]{:S(2)}) collective-permute-start(f32[5,132,2]{1,2,0:T(2,128)S(1)} %get-tuple-element.83), channel_id=1, source_target_pairs={{0,1},{1,2},{2,3},{3,4},{4,5},{5,6},{6,7},{8,9},{9,10},{10,11},{11... | collective-permute-start | bytes 15848 | tf_op jit(solution)/shard_map/ppermute | solution.py:37
  49.4 16.0 %collective-permute-start.13 = (f32[5,2,128]{1,2,0:T(8,128)S(1)}, f32[5,2,128]{1,2,0:T(8,128)S(1)}, u32[]{:S(2)}, u32[]{:S(2)}) collective-permute-start(f32[5,2,128]{1,2,0:T(8,128)S(1)} %get-tuple-element.125), channel_id=1, source_target_pairs={{8,0},{16,8},{24,16},{9,1},{17,9},{25,17},{10,2},{18,10},{26,18},{... | collective-permute-start | bytes 15368 | tf_op jit(solution)/shard_map/ppermute | solution.py:38
  50.7 14.7 %collective-permute-start.12 = (f32[5,2,128]{1,2,0:T(8,128)S(1)}, f32[5,2,128]{1,2,0:T(8,128)S(1)}, u32[]{:S(2)}, u32[]{:S(2)}) collective-permute-start(f32[5,2,128]{1,2,0:T(8,128)S(1)} %get-tuple-element.124), channel_id=1, source_target_pairs={{0,8},{8,16},{16,24},{1,9},{9,17},{17,25},{2,10},{10,18},{18,26},{... | collective-permute-start | bytes 15368 | tf_op jit(solution)/shard_map/ppermute | solution.py:37
  57.3 37.5 %all-to-all-start = ((f32[8,1,2]{2,1,0:T(1,128)}), f32[8,1,2]{2,1,0:T(1,128)S(1)}, u32[]{:S(2)}, u32[]{:S(2)}) async-start(f32[8,1,2]{2,1,0:T(1,128)} %bitcast.3), calls=%async_computation | async-start | bytes 8192 | tf_op jit(solution)/shard_map/all_to_all | solution.py:247
  65.5 10.9 %collective-permute-start.15 = (f32[5,132,2]{1,2,0:T(2,128)S(1)}, f32[5,132,2]{1,2,0:T(2,128)S(1)}, u32[]{:S(2)}, u32[]{:S(2)}) collective-permute-start(f32[5,132,2]{1,2,0:T(2,128)S(1)} %get-tuple-element.82), channel_id=1, source_target_pairs={{1,0},{2,1},{3,2},{4,3},{5,4},{6,5},{7,6},{9,8},{10,9},{11,10},{12... | collective-permute-start | bytes 15848 | tf_op jit(solution)/shard_map/ppermute | solution.py:38
  66.8 9.6 %collective-permute-start.14 = (f32[5,132,2]{1,2,0:T(2,128)S(1)}, f32[5,132,2]{1,2,0:T(2,128)S(1)}, u32[]{:S(2)}, u32[]{:S(2)}) collective-permute-start(f32[5,132,2]{1,2,0:T(2,128)S(1)} %get-tuple-element.81), channel_id=1, source_target_pairs={{0,1},{1,2},{2,3},{3,4},{4,5},{5,6},{6,7},{8,9},{9,10},{10,11},{11... | collective-permute-start | bytes 15848 | tf_op jit(solution)/shard_map/ppermute | solution.py:37
  79.1 9.1 %collective-permute-start.17 = (f32[5,2,128]{1,2,0:T(8,128)S(1)}, f32[5,2,128]{1,2,0:T(8,128)S(1)}, u32[]{:S(2)}, u32[]{:S(2)}) collective-permute-start(f32[5,2,128]{1,2,0:T(8,128)S(1)} %get-tuple-element.123), channel_id=1, source_target_pairs={{8,0},{16,8},{24,16},{9,1},{17,9},{25,17},{10,2},{18,10},{26,18},{... | collective-permute-start | bytes 15368 | tf_op jit(solution)/shard_map/ppermute | solution.py:38
  80.4 7.8 %collective-permute-start.16 = (f32[5,2,128]{1,2,0:T(8,128)S(1)}, f32[5,2,128]{1,2,0:T(8,128)S(1)}, u32[]{:S(2)}, u32[]{:S(2)}) collective-permute-start(f32[5,2,128]{1,2,0:T(8,128)S(1)} %get-tuple-element.122), channel_id=1, source_target_pairs={{0,8},{8,16},{16,24},{1,9},{9,17},{17,25},{2,10},{10,18},{18,26},{... | collective-permute-start | bytes 15368 | tf_op jit(solution)/shard_map/ppermute | solution.py:37
  88.3 13.2 %collective-permute-start.19 = (f32[5,132,2]{1,2,0:T(2,128)S(1)}, f32[5,132,2]{1,2,0:T(2,128)S(1)}, u32[]{:S(2)}, u32[]{:S(2)}) collective-permute-start(f32[5,132,2]{1,2,0:T(2,128)S(1)} %get-tuple-element.80), channel_id=1, source_target_pairs={{1,0},{2,1},{3,2},{4,3},{5,4},{6,5},{7,6},{9,8},{10,9},{11,10},{12... | collective-permute-start | bytes 15848 | tf_op jit(solution)/shard_map/ppermute | solution.py:38
  89.6 11.9 %collective-permute-start.18 = (f32[5,132,2]{1,2,0:T(2,128)S(1)}, f32[5,132,2]{1,2,0:T(2,128)S(1)}, u32[]{:S(2)}, u32[]{:S(2)}) collective-permute-start(f32[5,132,2]{1,2,0:T(2,128)S(1)} %get-tuple-element.79), channel_id=1, source_target_pairs={{0,1},{1,2},{2,3},{3,4},{4,5},{5,6},{6,7},{8,9},{9,10},{10,11},{11... | collective-permute-start | bytes 15848 | tf_op jit(solution)/shard_map/ppermute | solution.py:37
  94.8 20.3 %all-to-all-start.1 = ((f32[8,2,8,1024]{3,2,1,0:T(8,128)}), f32[8,2,8,1024]{3,2,1,0:T(8,128)}, u32[]{:S(2)}, u32[]{:S(2)}) async-start(f32[8,2,8,1024]{3,2,1,0:T(8,128)} %copy.183), calls=%async_computation.1 | async-start | bytes 1048576 | tf_op jit(solution)/shard_map/all_to_all | solution.py:240
  147.1 20.7 %all-to-all-start.2 = ((f32[8,2,8,1024]{3,1,2,0:T(2,128)}), f32[8,2,8,1024]{3,1,2,0:T(2,128)}, u32[]{:S(2)}, u32[]{:S(2)}) async-start(f32[8,2,8,1024]{3,1,2,0:T(2,128)} %constant_dynamic-update-slice_fusion), calls=%async_computation.2 | async-start | bytes 1048576 | tf_op jit(solution)/shard_map/all_to_all | solution.py:259
  (21 other events, 290.6 us)
where the time goes:
time: 176 us; the launch traced here: 174 us
  starting transfers between devices  79.3 us (45%)
  local copies, waits for them, and re-layouts  51.8 us (29%)
  other arithmetic  29.2 us (17%)
  waiting for transfers between devices  9.26 us (5%)
  matrix products  3.21 us (2%)
    ppermute x10, starting transfers between devices, padded(): before = lax.ppermute(last, axis, up)  47.2 us
    unnamed x79, local copies, waits for them, and re-layouts  28.2 us
    ppermute x10, starting transfers between devices, padded(): after = lax.ppermute(leading, axis, down)  12.9 us
    another operation x9, local copies, waits for them, and re-layouts, column_step(): jnp.stack([jnp.sum(cat_area * term_value, axis=1) for term_value in flux_...  8.24 us
    all_to_all x1, starting transfers between devices, local(): lax.all_to_all(flags.reshape(group_size, CAP), 'gy', split_axis=0, concat...  8.14 us
    all_to_all x1, starting transfers between devices, local(): lax.all_to_all(outgoing.reshape(group_size, CAP, POINT_QUANTITIES, TILE_P...  6.01 us
    all_to_all x1, starting transfers between devices, local(): lax.all_to_all(slot_fluxes.reshape(group_size, CAP, 8, TILE_POINTS), 'gy'...  5.09 us
    all_to_all x1, waiting for transfers between devices, local(): lax.all_to_all(outgoing.reshape(group_size, CAP, POINT_QUANTITIES, TILE_P...  4.93 us
  transfers between devices with their start and end apart: 23, of which 5 were waited for; matrix products, arithmetic and copies ran while one was open for 23% of the time, Pallas kernels for 0%

commit v1 on v0

v1 whole, which is shorter than its diff:
```python
import functools

import jax
import jax.numpy as jnp
from jax import lax
from jax.experimental import pallas as pl
from jax.experimental.pallas import tpu as pltpu
from jax.sharding import PartitionSpec as P

MESH = pl.DeviceIdType.MESH
BS = 32
BPX = 4
BPY = 4
CAP = 2
ICE = 7
SNOW = 3
LAYERS = 10
CLASSES = 5
SUB = 4
B = 16
TILE = 128
SENT = 6
BACK = 7
EVP = 10
HALO = 8
ROWS = TILE + 4 * HALO
VMEM_LIMIT = 48 * 1024 * 1024


def rcp(x):
    r = pl.reciprocal(x, approx=True)
    return r * (2.0 - x * r)


def swap_groups(x):
    group = lax.broadcasted_iota(jnp.int32, x[0].shape, 1) // BS
    even = (group % 2) == 0
    low = group < 2
    y = [None] * 4
    for a in (0, 2):
        y[a] = jnp.where(even, x[a], pltpu.roll(x[a + 1], BS, 1))
        y[a + 1] = jnp.where(even, pltpu.roll(x[a], TILE - BS, 1), x[a + 1])
    z = [None] * 4
    for a in (0, 1):
        z[a] = jnp.where(low, y[a], pltpu.roll(y[a + 2], 2 * BS, 1))
        z[a + 2] = jnp.where(low, pltpu.roll(y[a], 2 * BS, 1), y[a + 2])
    return z


def evp_steps(ext):
    bands = [2 * HALO * i + HALO for i in range((TILE + 2 * HALO) // (2 * HALO))]
    size = 2 * HALO
    third = 1.0 / 1.5

    def d_row(f, r):
        return 0.5 * (ext[f, r + 1 : r + 1 + size, :] - ext[f, r - 1 : r - 1 + size, :])

    def d_lane(x):
        width = x.shape[1]
        return 0.5 * (pltpu.roll(x, width - 1, 1) - pltpu.roll(x, 1, 1))

    def step(_, carry):
        for r in bands:
            here = slice(r, r + size)
            ux, uy = d_row(0, r), d_lane(ext[0, here, :])
            vx, vy = d_row(1, r), d_lane(ext[1, here, :])
            diverge, tension, shearing = ux + vy, ux - vy, uy + vx
            square = diverge * diverge + 0.25 * (tension * tension + shearing * shearing) + 0.04
            inverse = lax.rsqrt(square)
            push = ext[9, here, :]
            scaled = push * inverse
            ext[2, here, :] = third * ext[2, here, :] + (scaled * diverge - push)
            ext[3, here, :] = third * ext[3, here, :] + 0.25 * (scaled * tension)
            ext[4, here, :] = third * ext[4, here, :] + 0.125 * (scaled * shearing)
        for r in bands:
            here = slice(r, r + size)
            force_x = 0.5 * (d_row(2, r) + d_row(3, r)) + d_lane(ext[4, here, :])
            force_y = 0.5 * d_lane(ext[2, here, :] - ext[3, here, :]) + d_row(4, r)
            east, north = ext[0, here, :], ext[1, here, :]
            half, keep = ext[5, here, :], ext[6, here, :]
            ext[0, here, :] = keep * (east + 0.15 * north) + half * force_x + ext[7, here, :]
            ext[1, here, :] = keep * (north - 0.15 * east) + half * force_y + ext[8, here, :]
        return carry

    lax.fori_loop(0, SUB, step, 0)


def forward_kernel(
    n, m,
    cond, vel, stress, drive, weight, pressure, holder, marker,
    slots, vel_out, stress_out,
    blk, send, ext, pack_w, pack_e, top, bottom, got_w, got_e, got_t, got_b,
    send_sem, recv_sem, hsend_sem, hrecv_sem,
):
    gx, gy = lax.axis_index("gx"), lax.axis_index("gy")
    up, down = lax.rem(gx + m - 1, m), lax.rem(gx + 1, m)
    left, right = lax.rem(gy + n - 1, n), lax.rem(gy + 1, n)
    around = [(up, gy), (down, gy), (up, left), (up, right), (down, left), (down, right)]

    barrier = pltpu.get_barrier_semaphore()

    def greet(k, carry):
        pl.semaphore_signal(
            barrier, inc=1, device_id=(gx, lax.rem(gy + k, n)), device_id_type=MESH
        )
        return carry

    lax.fori_loop(1, n, greet, 0)
    for device in around:
        pl.semaphore_signal(barrier, inc=1, device_id=device, device_id_type=MESH)

    for bx in range(BPX):
        def part(f, q):
            return cond[f, pl.ds(BS * bx + q, 8, stride=4), :]

        for at, f in enumerate((0, 1, 2, None, 6, 7)):
            if f is None:
                pieces = [
                    0.25 * part(3, q) + 0.45 * part(4, q) + 0.3 * part(5, q) for q in range(4)
                ]
            else:
                pieces = [part(f, q) for q in range(4)]
            for by, piece in enumerate(swap_groups(pieces)):
                blk[bx * BPY + by, at] = piece

    def fill(o, carry):
        count = jnp.int32(0)
        first = jnp.int32(0)
        second = jnp.int32(0)
        for b in range(B):
            hit = jnp.where(holder[b, 0] == o, 1 - marker[b], 0)
            first = first + jnp.where(count == 0, hit * b, 0)
            second = second + jnp.where(count == 1, hit * b, 0)
            count = count + hit
        has_first = jnp.where(count > 0, 1.0, 0.0)
        has_second = jnp.where(count > 1, 1.0, 0.0)
        send[o, 0] = blk[first] * has_first
        send[o, 1] = blk[second] * has_second
        return carry

    lax.fori_loop(0, n, fill, 0)
    slots[gy] = send[gy]

    pl.semaphore_wait(barrier, n - 1 + len(around))

    def parcel(k):
        o = lax.rem(gy + k, n)
        return pltpu.make_async_remote_copy(
            src_ref=send.at[o], dst_ref=slots.at[gy],
            send_sem=send_sem.at[k], recv_sem=recv_sem.at[k],
            device_id=(gx, o), device_id_type=MESH,
        )

    def launch(k, carry):
        parcel(k).start()
        return carry

    lax.fori_loop(1, n, launch, 0)

    inner = slice(2 * HALO, 2 * HALO + TILE)
    ext[...] = jnp.zeros_like(ext)
    for f in range(2):
        ext[f, inner, :TILE] = vel[f]
    for f in range(3):
        ext[2 + f, inner, :TILE] = stress[f]
    column = lax.broadcasted_iota(jnp.int32, (BS, TILE), 1) // BS
    for bx in range(BPX):
        rows = slice(BS * bx, BS * bx + BS)
        into = slice(2 * HALO + BS * bx, 2 * HALO + BS * bx + BS)
        water = jnp.zeros((BS, TILE), jnp.float32)
        for by in range(BPY):
            sea = (1 - marker[bx * BPY + by]).astype(jnp.float32)
            water = jnp.where(column == by, sea, water)
        w = weight[rows, :]
        share = water * rcp(w + 0.5)
        half = 0.5 * share
        ext[5, into, :TILE] = half
        ext[6, into, :TILE] = share * w
        ext[7, into, :TILE] = half * (drive[0, rows, :] + drive[2, rows, :])
        ext[8, into, :TILE] = half * (drive[1, rows, :] + drive[3, rows, :])
        ext[9, into, :TILE] = pressure[rows, :] * (1.0 / 3.0)

    lane = lax.broadcasted_iota(jnp.int32, (TILE, TILE), 1)
    packed_w = jnp.zeros((TILE, TILE), jnp.float32)
    packed_e = jnp.zeros((TILE, TILE), jnp.float32)
    for f in range(EVP):
        own = (lane // HALO) == f
        x = ext[f, inner, :TILE]
        packed_w = jnp.where(own, pltpu.roll(x, HALO * f, 1) if f else x, packed_w)
        packed_e = jnp.where(own, pltpu.roll(x, HALO * (f + 1), 1), packed_e)
        top[f] = ext[f, 2 * HALO : 3 * HALO, :TILE]
        bottom[f] = ext[f, HALO + TILE : 2 * HALO + TILE, :TILE]
    pack_w[...] = packed_w
    pack_e[...] = packed_e

    head, tail = pl.ds(0, HALO), pl.ds(TILE - HALO, HALO)
    first, middle, last = pl.ds(0, HALO), pl.ds(HALO, TILE), pl.ds(HALO + TILE, HALO)
    halos = [
        (pack_w, got_e.at[middle], (gx, left)),
        (pack_e, got_w.at[middle], (gx, right)),
        (top, got_b, (up, gy)),
        (bottom, got_t, (down, gy)),
        (pack_w.at[head], got_e.at[last], (up, left)),
        (pack_e.at[head], got_w.at[last], (up, right)),
        (pack_w.at[tail], got_e.at[first], (down, left)),
        (pack_e.at[tail], got_w.at[first], (down, right)),
    ]
    copies = [
        pltpu.make_async_remote_copy(
            src_ref=src, dst_ref=dst, send_sem=hsend_sem.at[i], recv_sem=hrecv_sem.at[i],
            device_id=device, device_id_type=MESH,
        )
        for i, (src, dst, device) in enumerate(halos)
    ]
    for copy in copies:
        copy.start()
    for copy in copies:
        copy.wait()

    on_top = jnp.where(gx > 0, 1.0, 0.0)
    on_bottom = jnp.where(gx < m - 1, 1.0, 0.0)
    on_left = jnp.where(gy > 0, 1.0, 0.0)
    on_right = jnp.where(gy < n - 1, 1.0, 0.0)
    tall = TILE + 2 * HALO
    row = lax.broadcasted_iota(jnp.int32, (tall, TILE), 0)
    lane = lax.broadcasted_iota(jnp.int32, (tall, TILE), 1)
    upright = jnp.where(row < HALO, on_top, jnp.where(row < HALO + TILE, 1.0, on_bottom))
    sided_e = got_e[...] * (upright * on_right)
    sided_w = got_w[...] * (upright * on_left)
    for f in range(EVP):
        ext[f, HALO : 2 * HALO, :TILE] = got_t[f] * on_top
        ext[f, 2 * HALO + TILE : 3 * HALO + TILE, :TILE] = got_b[f] * on_bottom
        from_e = pltpu.roll(sided_e, TILE - HALO * f, 1) if f else sided_e
        from_w = pltpu.roll(sided_w, TILE - HALO * (f + 1), 1)
        ext[f, HALO : HALO + tall, TILE:] = jnp.where(
            lane < HALO, from_e, jnp.where(lane >= TILE - HALO, from_w, 0.0)
        )

    evp_steps(ext)
    for f in range(2):
        vel_out[f] = ext[f, inner, :TILE]
    for f in range(3):
        stress_out[f] = ext[2 + f, inner, :TILE]

    def finish(k, carry):
        parcel(k).wait()
        return carry

    lax.fori_loop(1, n, finish, 0)


def column_kernel(
    n, slots, warmth, share, thick, drift, warmth_out, fluxes,
    held, classes, in_sem, out_sem, class_sem,
):
    held5 = held.reshape(n * CAP, CLASSES, 8, 16, TILE)
    classes5 = classes.reshape(3, n * CAP, 8, 8, TILE)

    def class_copies():
        return [
            pltpu.make_async_copy(
                array.at[:, :, pl.ds(TILE * j, TILE)],
                classes5.at[i, :, j, pl.ds(0, CLASSES), :],
                class_sem.at[i, j],
            )
            for i, array in enumerate((share, thick, drift))
            for j in range(8)
        ]

    def moves(t, array, sem, out):
        group = pl.ds(CAP * t, CAP)
        copies = []
        for j in range(8):
            far = array.at[group, :, :, pl.ds(TILE * j, TILE)]
            near = held5.at[group, :, j, pl.ds(0, LAYERS), :]
            src, dst = (near, far) if out else (far, near)
            copies.append(pltpu.make_async_copy(src, dst, sem.at[t, j]))
        return copies

    for copy in class_copies():
        copy.start()

    def fetch(t, carry):
        for copy in moves(t, warmth, in_sem, False):
            copy.start()
        return carry

    lax.fori_loop(0, n, fetch, 0)
    for copy in class_copies():
        copy.wait()

    def one_slot(t, r):
        s = t * CAP + r
        ocean, salt, air, source, snowfall, wind = [slots[t, r, f] for f in range(SENT)]
        filled = salt > 0.25
        air_resist = rcp(1.0 + 2.0 * wind)
        sums = None
        for c in range(CLASSES):
            area, floe, lying = [
                classes[pl.ds(i * (n * CAP * 64) + s * 64 + c, 8, stride=8), :] for i in range(3)
            ]
            base = (s * CLASSES + c) * 128

            def place(l):
                return pl.ds(base + l, 8, stride=16)

            snow = lying + 0.3 * snowfall
            depth = floe * (1.0 / ICE)
            twice = 2.0 * depth
            snow_mass = snow * (2.0 / 3.0)
            snow_resist = snow * (1.0 / 0.9)
            snow_cond = rcp(snow_resist)
            top = rcp(0.5 * snow_resist + air_resist)
            above, resist = top, snow_resist
            ratios, values = [], []
            content = None
            for l in range(LAYERS):
                old = held[place(l), :]
                if l < SNOW:
                    mass = snow_mass
                else:
                    brine = salt * (0.2 + 0.1 * (l - SNOW))
                    mass = twice + twice * (0.2 * brine) * rcp(old * old + 0.1)
                if l < SNOW - 1:
                    below = snow_cond
                elif l < LAYERS - 1:
                    brine = salt * (0.2 + 0.1 * (l + 1 - SNOW))
                    shifted = held[place(l + 1), :] - 0.5
                    later = depth * shifted * rcp(2.0 * shifted + 0.1 * brine)
                    below = 2.0 * rcp(resist + later)
                    resist = later
                else:
                    below = 2.0 * rcp(resist)
                held_heat = mass * old
                content = held_heat if content is None else content + held_heat
                carried = held_heat
                pivot = mass + above + below
                if l == 0:
                    carried = carried + top * air + source
                if l == LAYERS - 1:
                    carried = carried + below * ocean
                if l > 0:
                    pivot = pivot - above * ratios[-1]
                    carried = carried + above * values[-1]
                inverse = rcp(pivot)
                ratios.append(below * inverse)
                values.append(carried * inverse)
                above = below
            new = values[-1]
            last = new
            held[place(LAYERS - 1), :] = jnp.where(filled, new, held[place(LAYERS - 1), :])
            for l in range(LAYERS - 2, -1, -1):
                new = values[l] + ratios[l] * new
                held[place(l), :] = jnp.where(filled, new, held[place(l), :])
            bottom_flux = below * (last - ocean)
            top_flux = top * (air - new)
            terms = [
                bottom_flux, top_flux, jnp.exp(-5.0 * lying - 1.5 * floe), new, snow, floe,
                0.05 * (content + top_flux - bottom_flux + source),
            ]
            terms = [area * term for term in terms]
            sums = terms if sums is None else [a + b for a, b in zip(sums, terms)]
        for f in range(BACK):
            fluxes[t, r, f] = sums[f]

    def tile(t, carry):
        for copy in moves(t, warmth, in_sem, False):
            copy.wait()
        for r in range(CAP):
            one_slot(t, r)
        for copy in moves(t, warmth_out, out_sem, True):
            copy.start()
        return carry

    lax.fori_loop(0, n, tile, 0)

    def flush(t, carry):
        for copy in moves(t, warmth_out, out_sem, True):
            copy.wait()
        return carry

    lax.fori_loop(0, n, flush, 0)


def return_kernel(n, fluxes, cond, holder, marker, out, got, send_sem, recv_sem):
    gx, gy = lax.axis_index("gx"), lax.axis_index("gy")
    barrier = pltpu.get_barrier_semaphore()

    def greet(k, carry):
        pl.semaphore_signal(
            barrier, inc=1, device_id=(gx, lax.rem(gy + k, n)), device_id_type=MESH
        )
        return carry

    lax.fori_loop(1, n, greet, 0)
    got[gy] = fluxes[gy]
    pl.semaphore_wait(barrier, n - 1)

    def parcel(k):
        o = lax.rem(gy + k, n)
        return pltpu.make_async_remote_copy(
            src_ref=fluxes.at[o], dst_ref=got.at[gy],
            send_sem=send_sem.at[k], recv_sem=recv_sem.at[k],
            device_id=(gx, o), device_id_type=MESH,
        )

    def launch(k, carry):
        parcel(k).start()
        return carry

    def finish(k, carry):
        parcel(k).wait()
        return carry

    lax.fori_loop(1, n, launch, 0)
    lax.fori_loop(1, n, finish, 0)

    for bx in range(BPX):
        pieces = []
        for by in range(BPY):
            b = bx * BPY + by
            rank = jnp.int32(0)
            for e in range(b):
                rank = rank + jnp.where(holder[e, 0] == holder[b, 0], 1 - marker[e], 0)
            sea = (1 - marker[b]).astype(jnp.float32)
            pieces.append(got[holder[b, 0], jnp.minimum(rank, CAP - 1)] * sea)
        parts = [swap_groups([piece[f] for piece in pieces]) for f in range(BACK)]
        for q in range(4):
            place = pl.ds(BS * bx + q, 8, stride=4)
            bottom_flux, top_flux, dim, warm, snow, floe, energy = [part[q] for part in parts]
            visible, snowfall, salt = cond[3, place, :], cond[6, place, :], cond[1, place, :]
            out[0, place, :] = bottom_flux
            out[1, place, :] = top_flux
            out[2, place, :] = 0.7 * visible * jnp.exp(-1.5 * snowfall) * dim
            out[3, place, :] = warm
            out[4, place, :] = snow
            out[5, place, :] = floe - 0.05 * bottom_flux
            out[6, place, :] = energy
            out[7, place, :] = -0.05 * bottom_flux * salt


def local(
    interface_conditions, level_warmth_profile, class_coverage_share, class_floe_depth,
    class_drift_depth, floe_drift_speed, internal_tension_tensor, external_drive,
    floe_weight, floe_pressure, holder_lookup, ground_tile_marker,
):
    n, m = lax.axis_size("gy"), lax.axis_size("gx")
    f32 = jnp.float32
    vmem = pl.BlockSpec(memory_space=pltpu.VMEM)
    smem = pl.BlockSpec(memory_space=pltpu.SMEM)
    hbm = pl.BlockSpec(memory_space=pl.ANY)
    shape = jax.ShapeDtypeStruct
    dma = pltpu.SemaphoreType.DMA
    slots, velocity, stress = pl.pallas_call(
        functools.partial(forward_kernel, n, m),
        out_shape=(
            shape((n, CAP, SENT, 8, TILE), f32),
            shape(floe_drift_speed.shape, f32),
            shape(internal_tension_tensor.shape, f32),
        ),
        in_specs=[vmem] * 6 + [smem] * 2,
        out_specs=(vmem,) * 3,
        scratch_shapes=[
            pltpu.VMEM((B, SENT, 8, TILE), f32),
            pltpu.VMEM((n, CAP, SENT, 8, TILE), f32),
            pltpu.VMEM((EVP, ROWS, 2 * TILE), f32),
            pltpu.VMEM((TILE, TILE), f32),
            pltpu.VMEM((TILE, TILE), f32),
            pltpu.VMEM((EVP, HALO, TILE), f32),
            pltpu.VMEM((EVP, HALO, TILE), f32),
            pltpu.VMEM((TILE + 2 * HALO, TILE), f32),
            pltpu.VMEM((TILE + 2 * HALO, TILE), f32),
            pltpu.VMEM((EVP, HALO, TILE), f32),
            pltpu.VMEM((EVP, HALO, TILE), f32),
            dma((n,)), dma((n,)), dma((8,)), dma((8,)),
        ],
        compiler_params=pltpu.CompilerParams(
            collective_id=0, has_side_effects=True, vmem_limit_bytes=VMEM_LIMIT
        ),
    )(
        interface_conditions, floe_drift_speed, internal_tension_tensor, external_drive,
        floe_weight, floe_pressure, holder_lookup, ground_tile_marker,
    )
    warmth, fluxes = pl.pallas_call(
        functools.partial(column_kernel, n),
        out_shape=(
            shape(level_warmth_profile.shape, f32),
            shape((n, CAP, BACK, 8, TILE), f32),
        ),
        in_specs=[vmem] + [hbm] * 4,
        out_specs=(hbm, vmem),
        scratch_shapes=[
            pltpu.VMEM((n * CAP * CLASSES * 8 * 16, TILE), f32),
            pltpu.VMEM((3 * n * CAP * 8 * 8, TILE), f32),
            dma((n, 8)), dma((n, 8)), dma((3, 8)),
        ],
        compiler_params=pltpu.CompilerParams(vmem_limit_bytes=VMEM_LIMIT),
    )(slots, level_warmth_profile, class_coverage_share, class_floe_depth, class_drift_depth)
    exchanges = pl.pallas_call(
        functools.partial(return_kernel, n),
        out_shape=shape(interface_conditions.shape, f32),
        in_specs=[vmem] * 2 + [smem] * 2,
        out_specs=vmem,
        scratch_shapes=[
            pltpu.VMEM((n, CAP, BACK, 8, TILE), f32),
            dma((n,)), dma((n,)),
        ],
        compiler_params=pltpu.CompilerParams(
            collective_id=1, has_side_effects=True, vmem_limit_bytes=VMEM_LIMIT
        ),
    )(fluxes, interface_conditions, holder_lookup, ground_tile_marker)
    return warmth, exchanges, velocity, stress


def solution(mesh):
    tile = P(None, "gx", "gy")
    owner = ("gx", "gy")
    return jax.shard_map(
        local,
        mesh=mesh,
        in_specs=(
            tile, P(owner, None, None, None), P(owner, None, None), P(owner, None, None),
            P(owner, None, None), tile, tile, tile, P("gx", "gy"), P("gx", "gy"),
            P(owner, None), P(owner),
        ),
        out_specs=(P(owner, None, None, None), tile, tile, tile),
        check_vma=False,
    )
```

time: 176 us -> 70.5 us (0.40)
  starting transfers between devices: 79.3 us -> 0 us
  Pallas kernels: 0 us -> 43.6 us
  other arithmetic: 29.2 us -> 0 us
  local copies, waits for them, and re-layouts: 51.8 us -> 25 us
  waiting for transfers between devices: 9.26 us -> 0 us
  matrix products: 3.21 us -> 0 us
    ppermute x20 -> x0, starting transfers between devices: 60.1 us -> none  [the longest x10 47.2 us: padded(): before = lax.ppermute(last, axis, up)]
    pallas_call x0 -> x3, Pallas kernels: none -> 43.6 us  [the longest x1 20.4 us: local(): pl.pallas_call(functools.partial(forward_kernel, n, m), out_shape=(shape(...]
    all_to_all x3 -> x0, starting transfers between devices: 19.2 us -> none  [the longest x1 8.14 us: local(): lax.all_to_all(flags.reshape(group_size, CAP), 'gy', split_axis=0, concat...]
    another operation x10 -> x0, local copies, waits for them, and re-layouts: 8.99 us -> none  [the longest x9 8.24 us: column_step(): jnp.stack([jnp.sum(cat_area * term_value, axis=1) for term_value in flux_...]
    mul x6 -> x0, other arithmetic: 6.95 us -> none  [the longest x1 4.02 us: column_step(): growth * salinity]
    all_to_all x3 -> x0, waiting for transfers between devices: 5.98 us -> none  [the longest x1 4.93 us: local(): lax.all_to_all(outgoing.reshape(group_size, CAP, POINT_QUANTITIES, TILE_P...]
    reshape x6 -> x0, local copies, waits for them, and re-layouts: 5.13 us -> none  [the longest x1 2.24 us: to_blocks(): shaped = tile_data.reshape(field_count, BPX, BS, BPY, BS)]
    select_n x1 -> x0, other arithmetic: 4.37 us -> none  [local(): jnp.where(occupied_mask[:, None, None, None] > 0.5, advanced_warmth, leve...]
  transfers between devices with their start and end apart: 23 -> 0, of which waited for: 5 -> 0; matrix products, arithmetic and copies ran while one was open for 23% -> 0% of each run, Pallas kernels for 0% -> 0%
where the time goes in v1:
time: 70.5 us; the launch traced here: 69.3 us
  Pallas kernels  43.6 us (62%)
  local copies, waits for them, and re-layouts  25 us (35%)
    unnamed x27, local copies, waits for them, and re-layouts  25 us
    pallas_call x1, Pallas kernels, local(): pl.pallas_call(functools.partial(forward_kernel, n, m), out_shape=(shape(...  20.4 us
    pallas_call x1, Pallas kernels, local(): pl.pallas_call(functools.partial(return_kernel, n), out_shape=shape(inter...  13.9 us
    pallas_call x1, Pallas kernels, local(): pl.pallas_call(functools.partial(column_kernel, n), out_shape=(shape(leve...  9.24 us

profile of v1, /device:TPU:0, one launch (start us, length us, event | category | flops | bytes accessed | tf_op | source)
XLA Modules:
  0.0 69.3 jit_solution(17591246469526788669)
XLA Ops:
  0.6 0.7 %copy.16.holder = s32[16,1]{1,0:T(8,128)S(1)} copy(s32[16,1]{0,1:T(1,128)} %param.22) | data formatting | bytes 128 | tf_op args[10]
  1.4 1.2 %copy.18.share = f32[16,5,1024]{2,1,0:T(8,128)S(1)} copy(f32[16,5,1024]{2,0,1:T(8,128)} %param.14) | data formatting | bytes 655360 | tf_op args[2]
  2.5 1.2 %copy.19.thick = f32[16,5,1024]{2,1,0:T(8,128)S(1)} copy(f32[16,5,1024]{2,0,1:T(8,128)} %param.15) | data formatting | bytes 655360 | tf_op args[3]
  3.7 1.2 %copy.20.drift = f32[16,5,1024]{2,1,0:T(8,128)S(1)} copy(f32[16,5,1024]{2,0,1:T(8,128)} %param.16) | data formatting | bytes 655360 | tf_op args[4]
  4.9 0.0 copy-start
  4.9 1.0 %copy-done = f32[8,128,128]{2,1,0:T(8,128)S(1)} copy-done((f32[8,128,128]{2,1,0:T(8,128)S(1)}, f32[8,128,128]{2,1,0:T(8,128)}, u32[]{:S(2)}) %copy-start) | copy-done | bytes 524312
  6.0 0.9 %copy-done.2 = f32[4,128,128]{2,1,0:T(8,128)S(1)} copy-done((f32[4,128,128]{2,1,0:T(8,128)S(1)}, f32[4,128,128]{2,1,0:T(8,128)}, u32[]{:S(2)}) %copy-start.2) | copy-done | bytes 262168
  6.9 0.9 %copy-done.3 = f32[3,128,128]{2,1,0:T(8,128)S(1)} copy-done((f32[3,128,128]{2,1,0:T(8,128)S(1)}, f32[3,128,128]{2,1,0:T(8,128)}, u32[]{:S(2)}) %copy-start.3) | copy-done | bytes 196632
  7.8 0.9 %copy-done.4 = f32[2,128,128]{2,1,0:T(8,128)S(1)} copy-done((f32[2,128,128]{2,1,0:T(8,128)S(1)}, f32[2,128,128]{2,1,0:T(8,128)}, u32[]{:S(2)}) %copy-start.4) | copy-done | bytes 131096
  8.7 0.8 %copy-done.5 = f32[128,128]{1,0:T(8,128)S(1)} copy-done((f32[128,128]{1,0:T(8,128)S(1)}, f32[128,128]{1,0:T(8,128)}, u32[]{:S(2)}) %copy-start.5) | copy-done | bytes 65560
  9.6 0.8 %copy-done.6 = f32[128,128]{1,0:T(8,128)S(1)} copy-done((f32[128,128]{1,0:T(8,128)S(1)}, f32[128,128]{1,0:T(8,128)}, u32[]{:S(2)}) %copy-start.6) | copy-done | bytes 65560
  10.4 0.7 copy-done.7
  11.1 20.4 %shard_map.147 = (f32[8,2,6,8,128]{4,3,2,1,0:T(8,128)S(1)}, f32[2,128,128]{2,1,0:T(8,128)S(1)}, f32[3,128,128]{2,1,0:T(8,128)S(1)}) custom-call(f32[8,128,128]{2,1,0:T(8,128)S(1)} %copy-done, f32[2,128,128]{2,1,0:T(8,128)S(1)} %copy-done.4, f32[3,128,128]{2,1,0:T(8,128)S(1)} %copy-done.3, f32[4,128,128]{2,1,0:T(8,128)S(1)} %copy-done.2, ...), custom_call_target="tpu_custom_call" | custom-call | tf_op jit(solution)/shard_map/pallas_call | solution.py:454
  31.5 6.2 %copy.17.warmth = f32[16,5,10,1024]{3,2,1,0:T(8,128)} copy(f32[16,5,10,1024]{3,0,2,1:T(8,128)} %param.13) | data formatting | bytes 6553600 | tf_op args[1]
  37.8 9.2 %shard_map.148 = (f32[16,5,10,1024]{3,2,1,0:T(8,128)}, f32[8,2,7,8,128]{4,3,2,1,0:T(8,128)S(1)}) custom-call(f32[8,2,6,8,128]{4,3,2,1,0:T(8,128)S(1)} %get-tuple-element.9.slots, f32[16,5,10,1024]{3,2,1,0:T(8,128)} %copy.17.warmth, f32[16,5,1024]{2,1,0:T(8,128)S(1)} %copy.18.share, f32[16,5,1024]{2,1,0:T(8,128)S(1)} %copy.19.thick, ...), custom_call_target="tpu_custom_call" | custom-call | tf_op jit(solution)/shard_map/pallas_call | solution.py:484
  47.0 0.0 copy-start.1
  47.0 0.0 copy-start.8
  47.0 6.2 %copy.22 = f32[16,5,10,1024]{3,0,2,1:T(8,128)} copy(f32[16,5,10,1024]{3,2,1,0:T(8,128)} %get-tuple-element.14) | data formatting | bytes 6553600
  53.2 0.0 copy-done.1
  53.2 0.0 copy-done.8
  53.2 13.9 %shard_map.149 = f32[8,128,128]{2,1,0:T(8,128)S(1)} custom-call(f32[8,2,7,8,128]{4,3,2,1,0:T(8,128)S(1)} %get-tuple-element.11.fluxes, f32[8,128,128]{2,1,0:T(8,128)S(1)} %copy-done.1, s32[16,1]{1,0:T(8,128)S(1)} %copy.16.holder, s32[16]{0:T(128)S(1)} %copy-done.8), custom_call_target="tpu_custom_call" | custom-call | tf_op jit(solution)/shard_map/pallas_call | solution.py:499
  67.2 0.8 %copy.26 = f32[8,128,128]{2,1,0:T(8,128)} copy(f32[8,128,128]{2,1,0:T(8,128)S(1)} %shard_map.149) | data formatting | bytes 1048576
  68.0 0.7 copy.27
  68.6 0.7 copy.28
  (6 shorter events, 0.0 us)
Async XLA Ops:
  4.9 1.0 %copy-start = (f32[8,128,128]{2,1,0:T(8,128)S(1)}, f32[8,128,128]{2,1,0:T(8,128)}, u32[]{:S(2)}) copy-start(f32[8,128,128]{2,1,0:T(8,128)} %cond.3) | copy-start | bytes 1572868
  6.0 0.9 %copy-start.2 = (f32[4,128,128]{2,1,0:T(8,128)S(1)}, f32[4,128,128]{2,1,0:T(8,128)}, u32[]{:S(2)}) copy-start(f32[4,128,128]{2,1,0:T(8,128)} %drive.1) | copy-start | bytes 786436
  6.9 0.9 %copy-start.3 = (f32[3,128,128]{2,1,0:T(8,128)S(1)}, f32[3,128,128]{2,1,0:T(8,128)}, u32[]{:S(2)}) copy-start(f32[3,128,128]{2,1,0:T(8,128)} %stress.1) | copy-start | bytes 589828
  7.8 0.9 %copy-start.4 = (f32[2,128,128]{2,1,0:T(8,128)S(1)}, f32[2,128,128]{2,1,0:T(8,128)}, u32[]{:S(2)}) copy-start(f32[2,128,128]{2,1,0:T(8,128)} %vel.1) | copy-start | bytes 393220
  8.7 0.8 %copy-start.5 = (f32[128,128]{1,0:T(8,128)S(1)}, f32[128,128]{1,0:T(8,128)}, u32[]{:S(2)}) copy-start(f32[128,128]{1,0:T(8,128)} %weight.1) | copy-start | bytes 196612
  9.6 0.8 %copy-start.6 = (f32[128,128]{1,0:T(8,128)S(1)}, f32[128,128]{1,0:T(8,128)}, u32[]{:S(2)}) copy-start(f32[128,128]{1,0:T(8,128)} %pressure.1) | copy-start | bytes 196612
  10.4 0.7 copy-start.7
  47.0 6.2 %copy-start.1 = (f32[8,128,128]{2,1,0:T(8,128)S(1)}, f32[8,128,128]{2,1,0:T(8,128)}, u32[]{:S(2)}) copy-start(f32[8,128,128]{2,1,0:T(8,128)} %cond.3) | copy-start | bytes 1572868
  47.0 6.2 %copy-start.8 = (s32[16]{0:T(128)S(1)}, s32[16]{0:T(128)}, u32[]{:S(2)}) copy-start(s32[16]{0:T(128)} %marker.3) | copy-start | bytes 196

commit v2 on v1

v2 whole, which is shorter than its diff:
```python
import functools

import jax
import jax.numpy as jnp
from jax import lax
from jax.experimental import pallas as pl
from jax.experimental.pallas import tpu as pltpu
from jax.sharding import PartitionSpec as P

MESH = pl.DeviceIdType.MESH
BS = 32
BPX = 4
BPY = 4
CAP = 2
ICE = 7
SNOW = 3
LAYERS = 10
CLASSES = 5
SUB = 4
B = 16
TILE = 128
SENT = 6
BACK = 5
EARLY = 2
EVP = 10
HALO = 8
ROWS = TILE + 4 * HALO
VMEM_LIMIT = 62 * 1024 * 1024


def rcp(x):
    r = pl.reciprocal(x, approx=True)
    return r * (2.0 - x * r)


def swap_groups(x):
    group = lax.broadcasted_iota(jnp.int32, x[0].shape, 1) // BS
    even = (group % 2) == 0
    low = group < 2
    y = [None] * 4
    for a in (0, 2):
        y[a] = jnp.where(even, x[a], pltpu.roll(x[a + 1], BS, 1))
        y[a + 1] = jnp.where(even, pltpu.roll(x[a], TILE - BS, 1), x[a + 1])
    z = [None] * 4
    for a in (0, 1):
        z[a] = jnp.where(low, y[a], pltpu.roll(y[a + 2], 2 * BS, 1))
        z[a + 2] = jnp.where(low, pltpu.roll(y[a], 2 * BS, 1), y[a + 2])
    return z


def evp_steps(ext):
    bands = [2 * HALO * i + HALO for i in range((TILE + 2 * HALO) // (2 * HALO))]
    size = 2 * HALO
    third = 1.0 / 1.5

    def d_row(f, r):
        return 0.5 * (ext[f, r + 1 : r + 1 + size, :] - ext[f, r - 1 : r - 1 + size, :])

    def d_lane(x):
        width = x.shape[1]
        return 0.5 * (pltpu.roll(x, width - 1, 1) - pltpu.roll(x, 1, 1))

    def step(_, carry):
        for r in bands:
            here = slice(r, r + size)
            ux, uy = d_row(0, r), d_lane(ext[0, here, :])
            vx, vy = d_row(1, r), d_lane(ext[1, here, :])
            diverge, tension, shearing = ux + vy, ux - vy, uy + vx
            square = diverge * diverge + 0.25 * (tension * tension + shearing * shearing) + 0.04
            inverse = lax.rsqrt(square)
            push = ext[9, here, :]
            scaled = push * inverse
            ext[2, here, :] = third * ext[2, here, :] + (scaled * diverge - push)
            ext[3, here, :] = third * ext[3, here, :] + 0.25 * (scaled * tension)
            ext[4, here, :] = third * ext[4, here, :] + 0.125 * (scaled * shearing)
        for r in bands:
            here = slice(r, r + size)
            force_x = 0.5 * (d_row(2, r) + d_row(3, r)) + d_lane(ext[4, here, :])
            force_y = 0.5 * d_lane(ext[2, here, :] - ext[3, here, :]) + d_row(4, r)
            east, north = ext[0, here, :], ext[1, here, :]
            half, keep = ext[5, here, :], ext[6, here, :]
            ext[0, here, :] = keep * (east + 0.15 * north) + half * force_x + ext[7, here, :]
            ext[1, here, :] = keep * (north - 0.15 * east) + half * force_y + ext[8, here, :]
        return carry

    lax.fori_loop(0, SUB, step, 0)


def parcels(n, gx, gy, rows, src, dst, send_sem, recv_sem):
    def sending(o):
        return pltpu.make_async_remote_copy(
            src_ref=src.at[pl.ds(o * rows, rows)], dst_ref=dst.at[pl.ds(gy * rows, rows)],
            send_sem=send_sem.at[o], recv_sem=recv_sem.at[gy],
            device_id=(gx, o), device_id_type=MESH,
        )

    def arriving(t):
        return pltpu.make_async_remote_copy(
            src_ref=src.at[pl.ds(t * rows, rows)], dst_ref=dst.at[pl.ds(t * rows, rows)],
            send_sem=send_sem.at[t], recv_sem=recv_sem.at[t],
            device_id=(gx, t), device_id_type=MESH,
        )

    return sending, arriving


def main_kernel(
    n, m,
    cond_far, vel_far, stress_far, drive_far, weight_far, pressure_far, holder, marker,
    warmth_far, share_far, thick_far, drift_far,
    new_far, got, got_early, coef, vel_out, stress_out,
    held, cond, vel, stress, drive, weight, pressure, share, thick, drift,
    blk, send, slots, early, fluxes,
    ext, pack_w, pack_e, top, bottom, got_w, got_e, got_t, got_b,
    in_sem, warm_sem, new_sem, send_sem, recv_sem, esend_sem, erecv_sem, fsend_sem, frecv_sem,
    hsend_sem, hrecv_sem,
):
    gx, gy = lax.axis_index("gx"), lax.axis_index("gy")
    up, down = lax.rem(gx + m - 1, m), lax.rem(gx + 1, m)
    left, right = lax.rem(gy + n - 1, n), lax.rem(gy + 1, n)
    around = [(up, gy), (down, gy), (up, left), (up, right), (down, left), (down, right)]
    groups = n * CAP // 8
    per_group = 8 // CAP
    reach = sorted(range(1, n), key=lambda k: abs(k - n // 2))

    pairs = (
        (cond_far, cond), (share_far, share), (thick_far, thick), (drift_far, drift),
        (vel_far, vel), (stress_far, stress), (drive_far, drive),
        (weight_far, weight), (pressure_far, pressure),
    )
    loads = [pltpu.make_async_copy(a, b, in_sem.at[i]) for i, (a, b) in enumerate(pairs)]

    def warm_load(g):
        at = pl.ds(pl.multiple_of(8 * g, 8), 8)
        return pltpu.make_async_copy(
            warmth_far.at[:, :, at, :], held.at[:, :, at, :], warm_sem.at[g]
        )

    def new_store(g):
        at = pl.ds(pl.multiple_of(8 * g, 8), 8)
        return pltpu.make_async_copy(
            held.at[:, :, at, :], new_far.at[:, :, at, :], new_sem.at[g]
        )

    loads[0].start()
    barrier = pltpu.get_barrier_semaphore()
    for k in reach:
        pl.semaphore_signal(
            barrier, inc=1, device_id=(gx, lax.rem(gy + k, n)), device_id_type=MESH
        )
    for device in around:
        pl.semaphore_signal(barrier, inc=1, device_id=device, device_id_type=MESH)
    for copy in loads[1:]:
        copy.start()
    for g in range(groups):
        warm_load(g).start()

    loads[0].wait()
    for bx in range(BPX):
        def part(f, q):
            return cond[f, pl.ds(BS * bx + q, 8, stride=4), :]

        for at, f in enumerate((0, 1, 2, None, 6, 7)):
            if f is None:
                pieces = [
                    0.25 * part(3, q) + 0.45 * part(4, q) + 0.3 * part(5, q) for q in range(4)
                ]
            else:
                pieces = [part(f, q) for q in range(4)]
            for by, piece in enumerate(swap_groups(pieces)):
                blk[bx * BPY + by, 8 * at : 8 * at + 8, :] = piece

    block_rows = SENT * 8

    def fill(o, carry):
        count = jnp.int32(0)
        first = jnp.int32(0)
        second = jnp.int32(0)
        for b in range(B):
            hit = jnp.where(holder[b] == o, 1 - marker[b], 0)
            first = first + jnp.where(count == 0, hit * b, 0)
            second = second + jnp.where(count == 1, hit * b, 0)
            count = count + hit
        has_first = jnp.where(count > 0, 1.0, 0.0)
        has_second = jnp.where(count > 1, 1.0, 0.0)
        at = pl.multiple_of(o * (CAP * block_rows), 8)
        send[pl.ds(at, block_rows), :] = blk[first] * has_first
        send[pl.ds(pl.multiple_of(at + block_rows, 8), block_rows), :] = blk[second] * has_second
        return carry

    lax.fori_loop(0, n, fill, 0)

    pl.semaphore_wait(barrier, n - 1 + len(around))

    sending, arriving = parcels(
        n, gx, gy, CAP * block_rows, send, slots, send_sem, recv_sem
    )
    for k in reach:
        sending(lax.rem(gy + k, n)).start()
    mine = pl.ds(pl.multiple_of(gy * (CAP * block_rows), 8), CAP * block_rows)
    slots[mine, :] = send[mine, :]

    for copy in loads[1:4]:
        copy.wait()

    def ahead(i, carry):
        g, j = i // 8, lax.rem(i, 8)
        at = pl.ds(pl.multiple_of(8 * g, 8), 8)
        cells = pl.ds(pl.multiple_of(TILE * j, TILE), TILE)
        dim = jnp.zeros((8, TILE), jnp.float32)
        floe = jnp.zeros((8, TILE), jnp.float32)
        for c in range(CLASSES):
            area, deep = share[c, at, cells], thick[c, at, cells]
            dim = dim + area * jnp.exp(-5.0 * drift[c, at, cells] - 1.5 * deep)
            floe = floe + area * deep
        early[pl.ds(g * (8 * 16) + j, 8, stride=16), :] = dim
        early[pl.ds(g * (8 * 16) + 8 + j, 8, stride=16), :] = floe
        return carry

    lax.fori_loop(0, groups * 8, ahead, 0)
    esending, earriving = parcels(
        n, gx, gy, CAP * EARLY * 8, early, got_early, esend_sem, erecv_sem
    )
    for k in reach:
        esending(lax.rem(gy + k, n)).start()
    mine_early = pl.ds(pl.multiple_of(gy * (CAP * EARLY * 8), 8), CAP * EARLY * 8)
    got_early[mine_early, :] = early[mine_early, :]

    for copy in loads[4:]:
        copy.wait()
    inner = slice(2 * HALO, 2 * HALO + TILE)
    ext[...] = jnp.zeros_like(ext)
    for f in range(2):
        ext[f, inner, :TILE] = vel[f]
    for f in range(3):
        ext[2 + f, inner, :TILE] = stress[f]
    column = lax.broadcasted_iota(jnp.int32, (BS, TILE), 1) // BS
    for bx in range(BPX):
        rows = slice(BS * bx, BS * bx + BS)
        into = slice(2 * HALO + BS * bx, 2 * HALO + BS * bx + BS)
        water = jnp.zeros((BS, TILE), jnp.float32)
        for by in range(BPY):
            sea = (1 - marker[bx * BPY + by]).astype(jnp.float32)
            water = jnp.where(column == by, sea, water)
        w = weight[rows, :]
        open_part = water * rcp(w + 0.5)
        half = 0.5 * open_part
        ext[5, into, :TILE] = half
        ext[6, into, :TILE] = open_part * w
        ext[7, into, :TILE] = half * (drive[0, rows, :] + drive[2, rows, :])
        ext[8, into, :TILE] = half * (drive[1, rows, :] + drive[3, rows, :])
        ext[9, into, :TILE] = pressure[rows, :] * (1.0 / 3.0)

    lane = lax.broadcasted_iota(jnp.int32, (TILE, TILE), 1)
    packed_w = jnp.zeros((TILE, TILE), jnp.float32)
    packed_e = jnp.zeros((TILE, TILE), jnp.float32)
    for f in range(EVP):
        own = (lane // HALO) == f
        x = ext[f, inner, :TILE]
        packed_w = jnp.where(own, pltpu.roll(x, HALO * f, 1) if f else x, packed_w)
        packed_e = jnp.where(own, pltpu.roll(x, HALO * (f + 1), 1), packed_e)
        top[f] = ext[f, 2 * HALO : 3 * HALO, :TILE]
        bottom[f] = ext[f, HALO + TILE : 2 * HALO + TILE, :TILE]
    pack_w[...] = packed_w
    pack_e[...] = packed_e

    head, tail = pl.ds(0, HALO), pl.ds(TILE - HALO, HALO)
    first, middle, last = pl.ds(0, HALO), pl.ds(HALO, TILE), pl.ds(HALO + TILE, HALO)
    halos = [
        (pack_w, got_e.at[middle], (gx, left)),
        (pack_e, got_w.at[middle], (gx, right)),
        (top, got_b, (up, gy)),
        (bottom, got_t, (down, gy)),
        (pack_w.at[head], got_e.at[last], (up, left)),
        (pack_e.at[head], got_w.at[last], (up, right)),
        (pack_w.at[tail], got_e.at[first], (down, left)),
        (pack_e.at[tail], got_w.at[first], (down, right)),
    ]
    copies = [
        pltpu.make_async_remote_copy(
            src_ref=src, dst_ref=dst, send_sem=hsend_sem.at[i], recv_sem=hrecv_sem.at[i],
            device_id=device, device_id_type=MESH,
        )
        for i, (src, dst, device) in enumerate(halos)
    ]
    for copy in copies:
        copy.start()
    coef[0] = 0.7 * cond[3] * jnp.exp(-1.5 * cond[6])
    coef[1] = -0.05 * cond[1]

    fsending, farriving = parcels(n, gx, gy, CAP * BACK * 8, fluxes, got, fsend_sem, frecv_sem)
    own_group = gy // per_group
    for i in range(groups):
        g = lax.rem(own_group + i, groups)
        for e in range(per_group):
            t = g * per_group + e

            @pl.when(t != gy)
            def _():
                arriving(t).wait_recv()

        warm_load(g).wait()

        def chunk(j, carry):
            column_step(g, j, slots, held, share, thick, drift, fluxes)
            return carry

        lax.fori_loop(0, 8, chunk, 0)
        new_store(g).start()
        for e in range(per_group):
            t = g * per_group + e

            @pl.when(t != gy)
            def _():
                fsending(t).start()

    mine_back = pl.ds(pl.multiple_of(gy * (CAP * BACK * 8), 8), CAP * BACK * 8)
    got[mine_back, :] = fluxes[mine_back, :]

    for copy in copies:
        copy.wait()
    on_top = jnp.where(gx > 0, 1.0, 0.0)
    on_bottom = jnp.where(gx < m - 1, 1.0, 0.0)
    on_left = jnp.where(gy > 0, 1.0, 0.0)
    on_right = jnp.where(gy < n - 1, 1.0, 0.0)
    tall = TILE + 2 * HALO
    row = lax.broadcasted_iota(jnp.int32, (tall, TILE), 0)
    lane = lax.broadcasted_iota(jnp.int32, (tall, TILE), 1)
    upright = jnp.where(row < HALO, on_top, jnp.where(row < HALO + TILE, 1.0, on_bottom))
    sided_e = got_e[...] * (upright * on_right)
    sided_w = got_w[...] * (upright * on_left)
    for f in range(EVP):
        ext[f, HALO : 2 * HALO, :TILE] = got_t[f] * on_top
        ext[f, 2 * HALO + TILE : 3 * HALO + TILE, :TILE] = got_b[f] * on_bottom
        from_e = pltpu.roll(sided_e, TILE - HALO * f, 1) if f else sided_e
        from_w = pltpu.roll(sided_w, TILE - HALO * (f + 1), 1)
        ext[f, HALO : HALO + tall, TILE:] = jnp.where(
            lane < HALO, from_e, jnp.where(lane >= TILE - HALO, from_w, 0.0)
        )

    evp_steps(ext)
    for f in range(2):
        vel_out[f] = ext[f, inner, :TILE]
    for f in range(3):
        stress_out[f] = ext[2 + f, inner, :TILE]

    for g in range(groups):
        new_store(g).wait()
    for k in reach:
        o = lax.rem(gy + k, n)
        sending(o).wait_send()
        esending(o).wait_send()
        earriving(o).wait_recv()
        fsending(o).wait_send()
        farriving(o).wait_recv()


def column_step(g, j, slots, held, share, thick, drift, fluxes):
    at = pl.ds(pl.multiple_of(8 * g, 8), 8)
    cells = pl.ds(pl.multiple_of(TILE * j, TILE), TILE)
    ocean, salt, air, source, snowfall, wind = [
        slots[pl.ds(g * (64 * SENT) + 8 * f + j, 8, stride=8 * SENT), :] for f in range(SENT)
    ]
    filled = salt > 0.25
    air_resist = rcp(1.0 + 2.0 * wind)
    sums = None
    for c in range(CLASSES):
        area, floe, lying = share[c, at, cells], thick[c, at, cells], drift[c, at, cells]
        snow = lying + 0.3 * snowfall
        depth = floe * (1.0 / ICE)
        twice = 2.0 * depth
        snow_mass = snow * (2.0 / 3.0)
        snow_resist = snow * (1.0 / 0.9)
        snow_cond = rcp(snow_resist)
        top = rcp(0.5 * snow_resist + air_resist)
        above, resist = top, snow_resist
        ratios, values = [], []
        content = None
        for l in range(LAYERS):
            old = held[c, l, at, cells]
            if l < SNOW:
                mass = snow_mass
            else:
                brine = salt * (0.2 + 0.1 * (l - SNOW))
                mass = twice + twice * (0.2 * brine) * rcp(old * old + 0.1)
            if l < SNOW - 1:
                below = snow_cond
            elif l < LAYERS - 1:
                brine = salt * (0.2 + 0.1 * (l + 1 - SNOW))
                shifted = held[c, l + 1, at, cells] - 0.5
                later = depth * shifted * rcp(2.0 * shifted + 0.1 * brine)
                below = 2.0 * rcp(resist + later)
                resist = later
            else:
                below = 2.0 * rcp(resist)
            held_heat = mass * old
            content = held_heat if content is None else content + held_heat
            carried = held_heat
            pivot = mass + above + below
            if l == 0:
                carried = carried + top * air + source
            if l == LAYERS - 1:
                carried = carried + below * ocean
            if l > 0:
                pivot = pivot - above * ratios[-1]
                carried = carried + above * values[-1]
            inverse = rcp(pivot)
            ratios.append(below * inverse)
            values.append(carried * inverse)
            above = below
        new = values[-1]
        last = new
        held[c, LAYERS - 1, at, cells] = jnp.where(filled, new, held[c, LAYERS - 1, at, cells])
        for l in range(LAYERS - 2, -1, -1):
            new = values[l] + ratios[l] * new
            held[c, l, at, cells] = jnp.where(filled, new, held[c, l, at, cells])
        bottom_flux = below * (last - ocean)
        top_flux = top * (air - new)
        terms = [
            bottom_flux, top_flux, new, snow,
            0.05 * (content + top_flux - bottom_flux + source),
        ]
        terms = [area * term for term in terms]
        sums = terms if sums is None else [a + b for a, b in zip(sums, terms)]
    for f in range(BACK):
        fluxes[pl.ds(g * (64 * BACK) + 8 * f + j, 8, stride=8 * BACK), :] = sums[f]


def output_kernel(
    n, held, got, got_early, coef, vel, stress, holder, marker,
    warmth_far, out_far, vel_far, stress_far, out, sem,
):
    copies = [
        pltpu.make_async_copy(a, b, sem.at[i])
        for i, (a, b) in enumerate(((held, warmth_far), (vel, vel_far), (stress, stress_far)))
    ]
    for copy in copies:
        copy.start()
    rows_back, rows_early = 8 * BACK, 8 * EARLY
    for bx in range(BPX):
        pieces = []
        for by in range(BPY):
            b = bx * BPY + by
            rank = jnp.int32(0)
            for e in range(b):
                rank = rank + jnp.where(holder[e] == holder[b], 1 - marker[e], 0)
            sea = (1 - marker[b]).astype(jnp.float32)
            s = holder[b] * CAP + jnp.minimum(rank, CAP - 1)
            one = [got[pl.ds(pl.multiple_of(s * rows_back + 8 * f, 8), 8), :] for f in range(BACK)]
            two = [
                got_early[pl.ds(pl.multiple_of(s * rows_early + 8 * f, 8), 8), :]
                for f in range(EARLY)
            ]
            pieces.append([x * sea for x in one + two])
        parts = [swap_groups([piece[f] for piece in pieces]) for f in range(BACK + EARLY)]
        for q in range(4):
            place = pl.ds(BS * bx + q, 8, stride=4)
            bottom_flux, top_flux, warm, snow, energy, dim, floe = [part[q] for part in parts]
            out[0, place, :] = bottom_flux
            out[1, place, :] = top_flux
            out[2, place, :] = coef[0, place, :] * dim
            out[3, place, :] = warm
            out[4, place, :] = snow
            out[5, place, :] = floe - 0.05 * bottom_flux
            out[6, place, :] = energy
            out[7, place, :] = coef[1, place, :] * bottom_flux
    last = pltpu.make_async_copy(out, out_far, sem.at[len(copies)])
    last.start()
    for copy in copies:
        copy.wait()
    last.wait()


def local(
    interface_conditions, level_warmth_profile, class_coverage_share, class_floe_depth,
    class_drift_depth, floe_drift_speed, internal_tension_tensor, external_drive,
    floe_weight, floe_pressure, holder_lookup, ground_tile_marker,
):
    n, m = lax.axis_size("gy"), lax.axis_size("gx")
    f32 = jnp.float32
    vmem = pl.BlockSpec(memory_space=pltpu.VMEM)
    smem = pl.BlockSpec(memory_space=pltpu.SMEM)
    hbm = pl.BlockSpec(memory_space=pltpu.HBM)
    shape = jax.ShapeDtypeStruct
    dma = pltpu.SemaphoreType.DMA
    holder = holder_lookup.reshape(-1)
    warmth = jnp.transpose(level_warmth_profile, (1, 2, 0, 3))
    share, thick, drift = [
        jnp.transpose(x, (1, 0, 2))
        for x in (class_coverage_share, class_floe_depth, class_drift_depth)
    ]
    places = n * CAP
    like = lambda x: pltpu.VMEM(x.shape, f32)
    held, got, got_early, coef, velocity, stress = pl.pallas_call(
        functools.partial(main_kernel, n, m),
        out_shape=(
            shape(warmth.shape, f32),
            shape((places * BACK * 8, TILE), f32),
            shape((places * EARLY * 8, TILE), f32),
            shape((2, TILE, TILE), f32),
            shape(floe_drift_speed.shape, f32),
            shape(internal_tension_tensor.shape, f32),
        ),
        in_specs=[hbm] * 6 + [smem] * 2 + [hbm] * 4,
        out_specs=(hbm,) + (vmem,) * 5,
        scratch_shapes=[
            like(warmth),
            like(interface_conditions), like(floe_drift_speed), like(internal_tension_tensor),
            like(external_drive), like(floe_weight), like(floe_pressure),
            like(share), like(thick), like(drift),
            pltpu.VMEM((B, SENT * 8, TILE), f32),
            pltpu.VMEM((places * SENT * 8, TILE), f32),
            pltpu.VMEM((places * SENT * 8, TILE), f32),
            pltpu.VMEM((places * EARLY * 8, TILE), f32),
            pltpu.VMEM((places * BACK * 8, TILE), f32),
            pltpu.VMEM((EVP, ROWS, 2 * TILE), f32),
            pltpu.VMEM((TILE, TILE), f32),
            pltpu.VMEM((TILE, TILE), f32),
            pltpu.VMEM((EVP, HALO, TILE), f32),
            pltpu.VMEM((EVP, HALO, TILE), f32),
            pltpu.VMEM((TILE + 2 * HALO, TILE), f32),
            pltpu.VMEM((TILE + 2 * HALO, TILE), f32),
            pltpu.VMEM((EVP, HALO, TILE), f32),
            pltpu.VMEM((EVP, HALO, TILE), f32),
            dma((9,)), dma((places // 8,)), dma((places // 8,)),
            dma((n,)), dma((n,)), dma((n,)), dma((n,)), dma((n,)), dma((n,)),
            dma((8,)), dma((8,)),
        ],
        compiler_params=pltpu.CompilerParams(
            collective_id=0, has_side_effects=True, vmem_limit_bytes=VMEM_LIMIT
        ),
    )(
        interface_conditions, floe_drift_speed, internal_tension_tensor, external_drive,
        floe_weight, floe_pressure, holder, ground_tile_marker, warmth, share, thick, drift,
    )
    warmth, exchanges, velocity, stress = pl.pallas_call(
        functools.partial(output_kernel, n),
        out_shape=tuple(
            shape(x.shape, f32) for x in (held, interface_conditions, velocity, stress)
        ),
        in_specs=[hbm] + [vmem] * 3 + [hbm] * 2 + [smem] * 2,
        out_specs=(hbm,) * 4,
        scratch_shapes=[like(interface_conditions), dma((4,))],
        compiler_params=pltpu.CompilerParams(vmem_limit_bytes=VMEM_LIMIT),
    )(held, got, got_early, coef, velocity, stress, holder, ground_tile_marker)
    return jnp.transpose(warmth, (2, 0, 1, 3)), exchanges, velocity, stress


def solution(mesh):
    tile = P(None, "gx", "gy")
    owner = ("gx", "gy")
    return jax.shard_map(
        local,
        mesh=mesh,
        in_specs=(
            tile, P(owner, None, None, None), P(owner, None, None), P(owner, None, None),
            P(owner, None, None), tile, tile, tile, P("gx", "gy"), P("gx", "gy"),
            P(owner, None), P(owner),
        ),
        out_specs=(P(owner, None, None, None), tile, tile, tile),
        check_vma=False,
    )
```

time: 70.5 us -> 142 us (2.01)
  Pallas kernels: 43.6 us -> 141 us
  local copies, waits for them, and re-layouts: 25 us -> 0 us
    pallas_call x3 -> x2, Pallas kernels: 43.6 us -> 141 us  [the longest x1 111 us: local(): pl.pallas_call(functools.partial(output_kernel, n), out_shape=tuple((shap...]
    unnamed x27 -> x0, local copies, waits for them, and re-layouts: 25 us -> none
where the time goes in v2:
time: 142 us
  Pallas kernels  141 us (99%)
    pallas_call x1, Pallas kernels, local(): pl.pallas_call(functools.partial(output_kernel, n), out_shape=tuple((shap...  111 us
    pallas_call x1, Pallas kernels, local(): pl.pallas_call(functools.partial(main_kernel, n, m), out_shape=(shape(war...  29.8 us

profile of v2, /device:TPU:0, one launch (start us, length us, event | category | flops | bytes accessed | tf_op | source)
XLA Modules:
  0.0 141.9 jit_solution(17978365967756345598)
XLA Ops:
  0.6 29.8 %shard_map.147 = (f32[5,10,16,1024]{3,2,1,0:T(8,128)}, f32[640,128]{1,0:T(8,128)}, f32[256,128]{1,0:T(8,128)}, f32[2,128,128]{2,1,0:T(8,128)}, f32[2,128,128]{2,1,0:T(8,128)}, /*index=5*/f32[3,128,128]{2,1,0:T(8,128)}) custom-call(f32[8,128,128]{2,1,0:T(8,128)} %cond_far.1, f32[2,128,128]{2,1,0:T(8,128)} %vel_far.1, f32[3,128,128]{2,1,0:T(8,128)} %stress_far.1, ...), custom_call_target="tpu_custom_call" | custom-call | tf_op jit(solution)/shard_map/pallas_call | solution.py:494
  30.5 111.4 %shard_map.148 = (f32[5,10,16,1024]{3,2,1,0:T(8,128)}, f32[8,128,128]{2,1,0:T(8,128)}, f32[2,128,128]{2,1,0:T(8,128)}, f32[3,128,128]{2,1,0:T(8,128)}) custom-call(f32[5,10,16,1024]{3,2,1,0:T(8,128)} %get-tuple-element.14.held, f32[640,128]{1,0:T(8,128)} %get-tuple-element.15.got, f32[256,128]{1,0:T(8,128)} %get-tuple-element.16.got_early, ...), custom_call_target="tpu_custom_call" | custom-call | tf_op jit(solution)/shard_map/pallas_call | solution.py:536

commit v3 on v2

--- a/solution.py
+++ b/solution.py
@@ -108,11 +108,11 @@
     n, m,
     cond_far, vel_far, stress_far, drive_far, weight_far, pressure_far, holder, marker,
     warmth_far, share_far, thick_far, drift_far,
-    new_far, got, got_early, coef, vel_out, stress_out,
-    held, cond, vel, stress, drive, weight, pressure, share, thick, drift,
+    new_far, got_far, early_far, coef_far, vel_out, stress_out,
+    held, got, got_early, coef, picks, cond, vel, stress, drive, weight, pressure, share, thick, drift,
     blk, send, slots, early, fluxes,
     ext, pack_w, pack_e, top, bottom, got_w, got_e, got_t, got_b,
-    in_sem, warm_sem, new_sem, send_sem, recv_sem, esend_sem, erecv_sem, fsend_sem, frecv_sem,
+    in_sem, warm_sem, new_sem, out_sem, send_sem, recv_sem, esend_sem, erecv_sem, fsend_sem, frecv_sem,
     hsend_sem, hrecv_sem,
 ):
     gx, gy = lax.axis_index("gx"), lax.axis_index("gy")
@@ -155,6 +155,21 @@
     for g in range(groups):
         warm_load(g).start()
 
+    def find(o, carry):
+        count = jnp.int32(0)
+        first = jnp.int32(0)
+        second = jnp.int32(0)
+        for b in range(B):
+            hit = jnp.where(holder[b] == o, 1 - marker[b], 0)
+            first = first + jnp.where(count == 0, hit * b, 0)
+            second = second + jnp.where(count == 1, hit * b, 0)
+            count = count + hit
+        picks[0, o] = first
+        picks[1, o] = second
+        picks[2, o] = count
+        return carry
+
+    lax.fori_loop(0, n, find, 0)
     loads[0].wait()
     for bx in range(BPX):
         def part(f, q):
@@ -173,14 +188,7 @@
     block_rows = SENT * 8
 
     def fill(o, carry):
-        count = jnp.int32(0)
-        first = jnp.int32(0)
-        second = jnp.int32(0)
-        for b in range(B):
-            hit = jnp.where(holder[b] == o, 1 - marker[b], 0)
-            first = first + jnp.where(count == 0, hit * b, 0)
-            second = second + jnp.where(count == 1, hit * b, 0)
-            count = count + hit
+        first, second, count = picks[0, o], picks[1, o], picks[2, o]
         has_first = jnp.where(count > 0, 1.0, 0.0)
         has_second = jnp.where(count > 1, 1.0, 0.0)
         at = pl.multiple_of(o * (CAP * block_rows), 8)
@@ -266,27 +274,39 @@
 
     head, tail = pl.ds(0, HALO), pl.ds(TILE - HALO, HALO)
     first, middle, last = pl.ds(0, HALO), pl.ds(HALO, TILE), pl.ds(HALO + TILE, HALO)
+    has_up, has_down, has_left, has_right = gx > 0, gx < m - 1, gy > 0, gy < n - 1
+    both = jnp.logical_and
     halos = [
-        (pack_w, got_e.at[middle], (gx, left)),
-        (pack_e, got_w.at[middle], (gx, right)),
-        (top, got_b, (up, gy)),
-        (bottom, got_t, (down, gy)),
-        (pack_w.at[head], got_e.at[last], (up, left)),
-        (pack_e.at[head], got_w.at[last], (up, right)),
-        (pack_w.at[tail], got_e.at[first], (down, left)),
-        (pack_e.at[tail], got_w.at[first], (down, right)),
+        (pack_w, got_e.at[middle], (gx, left), has_left, has_right),
+        (pack_e, got_w.at[middle], (gx, right), has_right, has_left),
+        (top, got_b, (up, gy), has_up, has_down),
+        (bottom, got_t, (down, gy), has_down, has_up),
+        (pack_w.at[head], got_e.at[last], (up, left), both(has_up, has_left),
+         both(has_down, has_right)),
+        (pack_e.at[head], got_w.at[last], (up, right), both(has_up, has_right),
+         both(has_down, has_left)),
+        (pack_w.at[tail], got_e.at[first], (down, left), both(has_down, has_left),
+         both(has_up, has_right)),
+        (pack_e.at[tail], got_w.at[first], (down, right), both(has_down, has_right),
+         both(has_up, has_left)),
     ]
-    copies = [
-        pltpu.make_async_remote_copy(
+
+    def halo(i):
+        src, dst, device = halos[i][:3]
+        return pltpu.make_async_remote_copy(
             src_ref=src, dst_ref=dst, send_sem=hsend_sem.at[i], recv_sem=hrecv_sem.at[i],
             device_id=device, device_id_type=MESH,
         )
-        for i, (src, dst, device) in enumerate(halos)
-    ]
-    for copy in copies:
-        copy.start()
+
+    for i in range(len(halos)):
+        @pl.when(halos[i][3])
+        def _():
+            halo(i).start()
     coef[0] = 0.7 * cond[3] * jnp.exp(-1.5 * cond[6])
     coef[1] = -0.05 * cond[1]
+    results = ((coef, coef_far), (vel, vel_out), (stress, stress_out), (got_early, early_far), (got, got_far))
+    stores = [pltpu.make_async_copy(a, b, out_sem.at[i]) for i, (a, b) in enumerate(results)]
+    stores[0].start()
 
     fsending, farriving = parcels(n, gx, gy, CAP * BACK * 8, fluxes, got, fsend_sem, frecv_sem)
     own_group = gy // per_group
@@ -317,21 +337,22 @@
     mine_back = pl.ds(pl.multiple_of(gy * (CAP * BACK * 8), 8), CAP * BACK * 8)
     got[mine_back, :] = fluxes[mine_back, :]
 
-    for copy in copies:
-        copy.wait()
-    on_top = jnp.where(gx > 0, 1.0, 0.0)
-    on_bottom = jnp.where(gx < m - 1, 1.0, 0.0)
-    on_left = jnp.where(gy > 0, 1.0, 0.0)
-    on_right = jnp.where(gy < n - 1, 1.0, 0.0)
+    for i in range(len(halos)):
+        @pl.when(halos[i][4])
+        def _():
+            halo(i).wait_recv()
+
     tall = TILE + 2 * HALO
     row = lax.broadcasted_iota(jnp.int32, (tall, TILE), 0)
     lane = lax.broadcasted_iota(jnp.int32, (tall, TILE), 1)
-    upright = jnp.where(row < HALO, on_top, jnp.where(row < HALO + TILE, 1.0, on_bottom))
-    sided_e = got_e[...] * (upright * on_right)
-    sided_w = got_w[...] * (upright * on_left)
+    upright = jnp.where(
+        row < HALO, gx, jnp.where(row < HALO + TILE, 1, m - 1 - gx)
+    )
+    sided_e = jnp.where(upright * (n - 1 - gy) > 0, got_e[...], 0.0)
+    sided_w = jnp.where(upright * gy > 0, got_w[...], 0.0)
     for f in range(EVP):
-        ext[f, HALO : 2 * HALO, :TILE] = got_t[f] * on_top
-        ext[f, 2 * HALO + TILE : 3 * HALO + TILE, :TILE] = got_b[f] * on_bottom
+        ext[f, HALO : 2 * HALO, :TILE] = jnp.where(has_up, got_t[f], 0.0)
+        ext[f, 2 * HALO + TILE : 3 * HALO + TILE, :TILE] = jnp.where(has_down, got_b[f], 0.0)
         from_e = pltpu.roll(sided_e, TILE - HALO * f, 1) if f else sided_e
         from_w = pltpu.roll(sided_w, TILE - HALO * (f + 1), 1)
         ext[f, HALO : HALO + tall, TILE:] = jnp.where(
@@ -340,19 +361,31 @@
 
     evp_steps(ext)
     for f in range(2):
-        vel_out[f] = ext[f, inner, :TILE]
+        vel[f] = ext[f, inner, :TILE]
     for f in range(3):
-        stress_out[f] = ext[2 + f, inner, :TILE]
-
+        stress[f] = ext[2 + f, inner, :TILE]
+    stores[1].start()
+    stores[2].start()
+
+    for k in reach:
+        earriving(lax.rem(gy + k, n)).wait_recv()
+    stores[3].start()
+    for k in reach:
+        farriving(lax.rem(gy + k, n)).wait_recv()
+    stores[4].start()
     for g in range(groups):
         new_store(g).wait()
+    for i in range(len(halos)):
+        @pl.when(halos[i][3])
+        def _():
+            halo(i).wait_send()
     for k in reach:
         o = lax.rem(gy + k, n)
         sending(o).wait_send()
         esending(o).wait_send()
-        earriving(o).wait_recv()
         fsending(o).wait_send()
-        farriving(o).wait_recv()
+    for copy in stores:
+        copy.wait()
 
 
 def column_step(g, j, slots, held, share, thick, drift, fluxes):
@@ -427,15 +460,27 @@
 
 
 def output_kernel(
-    n, held, got, got_early, coef, vel, stress, holder, marker,
-    warmth_far, out_far, vel_far, stress_far, out, sem,
+    n, new_far, got_far, early_far, coef_far, vel_from, stress_from, holder, marker,
+    warmth_far, out_far, vel_far, stress_far,
+    held, got, got_early, coef, vel, stress, out, load_sem, store_sem,
 ):
-    copies = [
-        pltpu.make_async_copy(a, b, sem.at[i])
-        for i, (a, b) in enumerate(((held, warmth_far), (vel, vel_far), (stress, stress_far)))
+    ways = [(got_far, got, None), (early_far, got_early, None), (coef_far, coef, None)]
+    for c in range(CLASSES):
+        ways.append((new_far.at[c], held.at[c], warmth_far.at[c]))
+    ways += [(vel_from, vel, vel_far), (stress_from, stress, stress_far)]
+    loads = [pltpu.make_async_copy(a, b, load_sem.at[i]) for i, (a, b, _) in enumerate(ways)]
+    stores = [
+        pltpu.make_async_copy(b, c, store_sem.at[i]) if c is not None else None
+        for i, (_, b, c) in enumerate(ways)
     ]
-    for copy in copies:
+    for copy in loads:
         copy.start()
+    for load, store in zip(loads[3:], stores[3:]):
+        load.wait()
+        store.start()
+    for copy in loads[:3]:
+        copy.wait()
+    bands = []
     rows_back, rows_early = 8 * BACK, 8 * EARLY
     for bx in range(BPX):
         pieces = []
@@ -464,11 +509,13 @@
             out[5, place, :] = floe - 0.05 * bottom_flux
             out[6, place, :] = energy
             out[7, place, :] = coef[1, place, :] * bottom_flux
-    last = pltpu.make_async_copy(out, out_far, sem.at[len(copies)])
-    last.start()
-    for copy in copies:
+        rows = pl.ds(BS * bx, BS)
+        bands.append(pltpu.make_async_copy(
+            out.at[:, rows, :], out_far.at[:, rows, :], store_sem.at[len(ways) + bx]
+        ))
+        bands[-1].start()
+    for copy in stores[3:] + bands:
         copy.wait()
-    last.wait()
 
 
 def local(
@@ -478,7 +525,6 @@
 ):
     n, m = lax.axis_size("gy"), lax.axis_size("gx")
     f32 = jnp.float32
-    vmem = pl.BlockSpec(memory_space=pltpu.VMEM)
     smem = pl.BlockSpec(memory_space=pltpu.SMEM)
     hbm = pl.BlockSpec(memory_space=pltpu.HBM)
     shape = jax.ShapeDtypeStruct
@@ -502,9 +548,13 @@
             shape(internal_tension_tensor.shape, f32),
         ),
         in_specs=[hbm] * 6 + [smem] * 2 + [hbm] * 4,
-        out_specs=(hbm,) + (vmem,) * 5,
+        out_specs=(hbm,) * 6,
         scratch_shapes=[
             like(warmth),
+            pltpu.VMEM((places * BACK * 8, TILE), f32),
+            pltpu.VMEM((places * EARLY * 8, TILE), f32),
+            pltpu.VMEM((2, TILE, TILE), f32),
+            pltpu.SMEM((3, n), jnp.int32),
             like(interface_conditions), like(floe_drift_speed), like(internal_tension_tensor),
             like(external_drive), like(floe_weight), like(floe_pressure),
             like(share), like(thick), like(drift),
@@ -522,7 +572,7 @@
             pltpu.VMEM((TILE + 2 * HALO, TILE), f32),
             pltpu.VMEM((EVP, HALO, TILE), f32),
             pltpu.VMEM((EVP, HALO, TILE), f32),
-            dma((9,)), dma((places // 8,)), dma((places // 8,)),
+            dma((9,)), dma((places // 8,)), dma((places // 8,)), dma((5,)),
             dma((n,)), dma((n,)), dma((n,)), dma((n,)), dma((n,)), dma((n,)),
             dma((8,)), dma((8,)),
         ],
@@ -538,9 +588,12 @@
         out_shape=tuple(
             shape(x.shape, f32) for x in (held, interface_conditions, velocity, stress)
         ),
-        in_specs=[hbm] + [vmem] * 3 + [hbm] * 2 + [smem] * 2,
+        in_specs=[hbm] * 6 + [smem] * 2,
         out_specs=(hbm,) * 4,
-        scratch_shapes=[like(interface_conditions), dma((4,))],
+        scratch_shapes=[
+            like(held), like(got), like(got_early), like(coef), like(velocity), like(stress),
+            like(interface_conditions), dma((CLASSES + 5,)), dma((CLASSES + 5 + BPX,)),
+        ],
         compiler_params=pltpu.CompilerParams(vmem_limit_bytes=VMEM_LIMIT),
     )(held, got, got_early, coef, velocity, stress, holder, ground_tile_marker)
     return jnp.transpose(warmth, (2, 0, 1, 3)), exchanges, velocity, stress

time: 142 us -> 35.2 us (0.25)
  Pallas kernels: 141 us -> 34.3 us
    pallas_call x1, Pallas kernels: 111 us -> 4.72 us  [local(): pl.pallas_call(functools.partial(output_kernel, n), out_shape=tuple((shap...]
where the time goes in v3:
time: 35.2 us; the launch traced here: 35 us
  Pallas kernels  34.3 us (97%)
  between operations  0.64 us (2%)
    pallas_call x1, Pallas kernels, local(): pl.pallas_call(functools.partial(main_kernel, n, m), out_shape=(shape(war...  29.6 us
    pallas_call x1, Pallas kernels, local(): pl.pallas_call(functools.partial(output_kernel, n), out_shape=tuple((shap...  4.72 us

profile of v3, /device:TPU:0, one launch (start us, length us, event | category | flops | bytes accessed | tf_op | source)
XLA Modules:
  0.0 35.0 jit_solution(12919778730634642791)
XLA Ops:
  0.6 29.6 %shard_map.147 = (f32[5,10,16,1024]{3,2,1,0:T(8,128)}, f32[640,128]{1,0:T(8,128)}, f32[256,128]{1,0:T(8,128)}, f32[2,128,128]{2,1,0:T(8,128)}, f32[2,128,128]{2,1,0:T(8,128)}, /*index=5*/f32[3,128,128]{2,1,0:T(8,128)}) custom-call(f32[8,128,128]{2,1,0:T(8,128)} %cond_far.1, f32[2,128,128]{2,1,0:T(8,128)} %vel_far.1, f32[3,128,128]{2,1,0:T(8,128)} %stress_far.1, ...), custom_call_target="tpu_custom_call" | custom-call | tf_op jit(solution)/shard_map/pallas_call | solution.py:540
  30.2 4.7 %shard_map.148 = (f32[5,10,16,1024]{3,2,1,0:T(8,128)}, f32[8,128,128]{2,1,0:T(8,128)}, f32[2,128,128]{2,1,0:T(8,128)}, f32[3,128,128]{2,1,0:T(8,128)}) custom-call(f32[5,10,16,1024]{3,2,1,0:T(8,128)} %get-tuple-element.14.new_far, f32[640,128]{1,0:T(8,128)} %get-tuple-element.15.got_far, f32[256,128]{1,0:T(8,128)} %get-tuple-element.16.early_far, ...), custom_call_target="tpu_custom_call" | custom-call | tf_op jit(solution)/shard_map/pallas_call | solution.py:586

commit v4 on v3

--- a/solution.py
+++ b/solution.py
@@ -29,8 +29,7 @@
 
 
 def rcp(x):
-    r = pl.reciprocal(x, approx=True)
-    return r * (2.0 - x * r)
+    return pl.reciprocal(x, approx=True)
 
 
 def swap_groups(x):
@@ -196,15 +195,16 @@
         send[pl.ds(pl.multiple_of(at + block_rows, 8), block_rows), :] = blk[second] * has_second
         return carry
 
-    lax.fori_loop(0, n, fill, 0)
-
     pl.semaphore_wait(barrier, n - 1 + len(around))
 
     sending, arriving = parcels(
         n, gx, gy, CAP * block_rows, send, slots, send_sem, recv_sem
     )
     for k in reach:
-        sending(lax.rem(gy + k, n)).start()
+        o = lax.rem(gy + k, n)
+        fill(o, 0)
+        sending(o).start()
+    fill(gy, 0)
     mine = pl.ds(pl.multiple_of(gy * (CAP * block_rows), 8), CAP * block_rows)
     slots[mine, :] = send[mine, :]
 
@@ -229,8 +229,6 @@
     esending, earriving = parcels(
         n, gx, gy, CAP * EARLY * 8, early, got_early, esend_sem, erecv_sem
     )
-    for k in reach:
-        esending(lax.rem(gy + k, n)).start()
     mine_early = pl.ds(pl.multiple_of(gy * (CAP * EARLY * 8), 8), CAP * EARLY * 8)
     got_early[mine_early, :] = early[mine_early, :]
 
@@ -319,6 +317,9 @@
             def _():
                 arriving(t).wait_recv()
 
+        if i == min(1, groups - 1):
+            for k in reach:
+                esending(lax.rem(gy + k, n)).start()
         warm_load(g).wait()
 
         def chunk(j, carry):
@@ -475,22 +476,22 @@
     ]
     for copy in loads:
         copy.start()
-    for load, store in zip(loads[3:], stores[3:]):
-        load.wait()
-        store.start()
+    bands = []
+    spots = []
+    for b in range(B):
+        rank = jnp.int32(0)
+        for e in range(b):
+            rank = rank + jnp.where(holder[e] == holder[b], 1 - marker[e], 0)
+        spots.append(holder[b] * CAP + jnp.minimum(rank, CAP - 1))
     for copy in loads[:3]:
         copy.wait()
-    bands = []
     rows_back, rows_early = 8 * BACK, 8 * EARLY
     for bx in range(BPX):
         pieces = []
         for by in range(BPY):
             b = bx * BPY + by
-            rank = jnp.int32(0)
-            for e in range(b):
-                rank = rank + jnp.where(holder[e] == holder[b], 1 - marker[e], 0)
             sea = (1 - marker[b]).astype(jnp.float32)
-            s = holder[b] * CAP + jnp.minimum(rank, CAP - 1)
+            s = spots[b]
             one = [got[pl.ds(pl.multiple_of(s * rows_back + 8 * f, 8), 8), :] for f in range(BACK)]
             two = [
                 got_early[pl.ds(pl.multiple_of(s * rows_early + 8 * f, 8), 8), :]
@@ -514,6 +515,9 @@
             out.at[:, rows, :], out_far.at[:, rows, :], store_sem.at[len(ways) + bx]
         ))
         bands[-1].start()
+        for at in range(3 + bx, len(ways), BPX):
+            loads[at].wait()
+            stores[at].start()
     for copy in stores[3:] + bands:
         copy.wait()
 

time: 35.2 us -> 34.7 us (0.986)
  Pallas kernels: 34.3 us -> 33.9 us
    pallas_call x1, Pallas kernels: 29.6 us -> 29.2 us  [local(): pl.pallas_call(functools.partial(main_kernel, n, m), out_shape=(shape(war...]
where the time goes in v4:
time: 34.7 us; the launch traced here: 34.5 us
  Pallas kernels  33.9 us (98%)
  between operations  0.64 us (2%)
    pallas_call x1, Pallas kernels, local(): pl.pallas_call(functools.partial(main_kernel, n, m), out_shape=(shape(war...  29.2 us
    pallas_call x1, Pallas kernels, local(): pl.pallas_call(functools.partial(output_kernel, n), out_shape=tuple((shap...  4.73 us

profile of v4, /device:TPU:0, one launch (start us, length us, event | category | flops | bytes accessed | tf_op | source)
XLA Modules:
  0.0 34.5 jit_solution(5545160919028834365)
XLA Ops:
  0.6 29.2 %shard_map.147 = (f32[5,10,16,1024]{3,2,1,0:T(8,128)}, f32[640,128]{1,0:T(8,128)}, f32[256,128]{1,0:T(8,128)}, f32[2,128,128]{2,1,0:T(8,128)}, f32[2,128,128]{2,1,0:T(8,128)}, /*index=5*/f32[3,128,128]{2,1,0:T(8,128)}) custom-call(f32[8,128,128]{2,1,0:T(8,128)} %cond_far.1, f32[2,128,128]{2,1,0:T(8,128)} %vel_far.1, f32[3,128,128]{2,1,0:T(8,128)} %stress_far.1, ...), custom_call_target="tpu_custom_call" | custom-call | tf_op jit(solution)/shard_map/pallas_call | solution.py:544
  29.8 4.7 %shard_map.148 = (f32[5,10,16,1024]{3,2,1,0:T(8,128)}, f32[8,128,128]{2,1,0:T(8,128)}, f32[2,128,128]{2,1,0:T(8,128)}, f32[3,128,128]{2,1,0:T(8,128)}) custom-call(f32[5,10,16,1024]{3,2,1,0:T(8,128)} %get-tuple-element.14.new_far, f32[640,128]{1,0:T(8,128)} %get-tuple-element.15.got_far, f32[256,128]{1,0:T(8,128)} %get-tuple-element.16.early_far, ...), custom_call_target="tpu_custom_call" | custom-call | tf_op jit(solution)/shard_map/pallas_call | solution.py:590

commit v5 on v4

--- a/solution.py
+++ b/solution.py
@@ -111,7 +111,7 @@
     held, got, got_early, coef, picks, cond, vel, stress, drive, weight, pressure, share, thick, drift,
     blk, send, slots, early, fluxes,
     ext, pack_w, pack_e, top, bottom, got_w, got_e, got_t, got_b,
-    in_sem, warm_sem, new_sem, out_sem, send_sem, recv_sem, esend_sem, erecv_sem, fsend_sem, frecv_sem,
+    in_sem, band_sem, warm_sem, new_sem, out_sem, got_sem, send_sem, recv_sem, esend_sem, erecv_sem, fsend_sem, frecv_sem,
     hsend_sem, hrecv_sem,
 ):
     gx, gy = lax.axis_index("gx"), lax.axis_index("gy")
@@ -123,7 +123,7 @@
     reach = sorted(range(1, n), key=lambda k: abs(k - n // 2))
 
     pairs = (
-        (cond_far, cond), (share_far, share), (thick_far, thick), (drift_far, drift),
+        (share_far, share), (thick_far, thick), (drift_far, drift),
         (vel_far, vel), (stress_far, stress), (drive_far, drive),
         (weight_far, weight), (pressure_far, pressure),
     )
@@ -141,7 +141,13 @@
             held.at[:, :, at, :], new_far.at[:, :, at, :], new_sem.at[g]
         )
 
-    loads[0].start()
+    field_loads = []
+    for bx in range(BPX):
+        rows = pl.ds(BS * bx, BS)
+        field_loads.append(pltpu.make_async_copy(
+            cond_far.at[:, rows, :], cond.at[:, rows, :], band_sem.at[bx]
+        ))
+        field_loads[-1].start()
     barrier = pltpu.get_barrier_semaphore()
     for k in reach:
         pl.semaphore_signal(
@@ -149,7 +155,7 @@
         )
     for device in around:
         pl.semaphore_signal(barrier, inc=1, device_id=device, device_id_type=MESH)
-    for copy in loads[1:]:
+    for copy in loads:
         copy.start()
     for g in range(groups):
         warm_load(g).start()
@@ -169,8 +175,9 @@
         return carry
 
     lax.fori_loop(0, n, find, 0)
-    loads[0].wait()
     for bx in range(BPX):
+        field_loads[bx].wait()
+
         def part(f, q):
             return cond[f, pl.ds(BS * bx + q, 8, stride=4), :]
 
@@ -208,7 +215,7 @@
     mine = pl.ds(pl.multiple_of(gy * (CAP * block_rows), 8), CAP * block_rows)
     slots[mine, :] = send[mine, :]
 
-    for copy in loads[1:4]:
+    for copy in loads[:3]:
         copy.wait()
 
     def ahead(i, carry):
@@ -232,7 +239,7 @@
     mine_early = pl.ds(pl.multiple_of(gy * (CAP * EARLY * 8), 8), CAP * EARLY * 8)
     got_early[mine_early, :] = early[mine_early, :]
 
-    for copy in loads[4:]:
+    for copy in loads[3:]:
         copy.wait()
     inner = slice(2 * HALO, 2 * HALO + TILE)
     ext[...] = jnp.zeros_like(ext)
@@ -302,7 +309,7 @@
             halo(i).start()
     coef[0] = 0.7 * cond[3] * jnp.exp(-1.5 * cond[6])
     coef[1] = -0.05 * cond[1]
-    results = ((coef, coef_far), (vel, vel_out), (stress, stress_out), (got_early, early_far), (got, got_far))
+    results = ((coef, coef_far), (vel, vel_out), (stress, stress_out), (got_early, early_far))
     stores = [pltpu.make_async_copy(a, b, out_sem.at[i]) for i, (a, b) in enumerate(results)]
     stores[0].start()
 
@@ -371,9 +378,17 @@
     for k in reach:
         earriving(lax.rem(gy + k, n)).wait_recv()
     stores[3].start()
-    for k in reach:
-        farriving(lax.rem(gy + k, n)).wait_recv()
-    stores[4].start()
+    back_rows = CAP * BACK * 8
+
+    def got_store(t):
+        at = pl.ds(pl.multiple_of(t * back_rows, 8), back_rows)
+        return pltpu.make_async_copy(got.at[at], got_far.at[at], got_sem.at[t])
+
+    got_store(gy).start()
+    for k in reversed(reach):
+        t = lax.rem(gy + k, n)
+        farriving(t).wait_recv()
+        got_store(t).start()
     for g in range(groups):
         new_store(g).wait()
     for i in range(len(halos)):
@@ -387,6 +402,8 @@
         fsending(o).wait_send()
     for copy in stores:
         copy.wait()
+    for t in range(n):
+        got_store(t).wait()
 
 
 def column_step(g, j, slots, held, share, thick, drift, fluxes):
@@ -467,7 +484,9 @@
 ):
     ways = [(got_far, got, None), (early_far, got_early, None), (coef_far, coef, None)]
     for c in range(CLASSES):
-        ways.append((new_far.at[c], held.at[c], warmth_far.at[c]))
+        for h in range(2):
+            half = pl.ds(h * (LAYERS // 2), LAYERS // 2)
+            ways.append((new_far.at[c, half], held.at[c, half], warmth_far.at[c, half]))
     ways += [(vel_from, vel, vel_far), (stress_from, stress, stress_far)]
     loads = [pltpu.make_async_copy(a, b, load_sem.at[i]) for i, (a, b, _) in enumerate(ways)]
     stores = [
@@ -576,7 +595,7 @@
             pltpu.VMEM((TILE + 2 * HALO, TILE), f32),
             pltpu.VMEM((EVP, HALO, TILE), f32),
             pltpu.VMEM((EVP, HALO, TILE), f32),
-            dma((9,)), dma((places // 8,)), dma((places // 8,)), dma((5,)),
+            dma((8,)), dma((BPX,)), dma((places // 8,)), dma((places // 8,)), dma((4,)), dma((n,)),
             dma((n,)), dma((n,)), dma((n,)), dma((n,)), dma((n,)), dma((n,)),
             dma((8,)), dma((8,)),
         ],
@@ -596,7 +615,7 @@
         out_specs=(hbm,) * 4,
         scratch_shapes=[
             like(held), like(got), like(got_early), like(coef), like(velocity), like(stress),
-            like(interface_conditions), dma((CLASSES + 5,)), dma((CLASSES + 5 + BPX,)),
+            like(interface_conditions), dma((2 * CLASSES + 5,)), dma((2 * CLASSES + 5 + BPX,)),
         ],
         compiler_params=pltpu.CompilerParams(vmem_limit_bytes=VMEM_LIMIT),
     )(held, got, got_early, coef, velocity, stress, holder, ground_tile_marker)

time: 34.7 us -> 34.8 us (level)
  no operation moved by 1% of the time
where the time goes in v5:
time: 34.8 us; the launch traced here: 34.6 us
  Pallas kernels  33.9 us (97%)
  between operations  0.64 us (2%)
    pallas_call x1, Pallas kernels, local(): pl.pallas_call(functools.partial(main_kernel, n, m), out_shape=(shape(war...  29.2 us
    pallas_call x1, Pallas kernels, local(): pl.pallas_call(functools.partial(output_kernel, n), out_shape=tuple((shap...  4.74 us

profile of v5, /device:TPU:0, one launch (start us, length us, event | category | flops | bytes accessed | tf_op | source)
XLA Modules:
  0.0 34.6 jit_solution(5705431396089576569)
XLA Ops:
  0.6 29.2 %shard_map.147 = (f32[5,10,16,1024]{3,2,1,0:T(8,128)}, f32[640,128]{1,0:T(8,128)}, f32[256,128]{1,0:T(8,128)}, f32[2,128,128]{2,1,0:T(8,128)}, f32[2,128,128]{2,1,0:T(8,128)}, /*index=5*/f32[3,128,128]{2,1,0:T(8,128)}) custom-call(f32[8,128,128]{2,1,0:T(8,128)} %cond_far.1, f32[2,128,128]{2,1,0:T(8,128)} %vel_far.1, f32[3,128,128]{2,1,0:T(8,128)} %stress_far.1, ...), custom_call_target="tpu_custom_call" | custom-call | tf_op jit(solution)/shard_map/pallas_call | solution.py:563
  29.8 4.7 %shard_map.148 = (f32[5,10,16,1024]{3,2,1,0:T(8,128)}, f32[8,128,128]{2,1,0:T(8,128)}, f32[2,128,128]{2,1,0:T(8,128)}, f32[3,128,128]{2,1,0:T(8,128)}) custom-call(f32[5,10,16,1024]{3,2,1,0:T(8,128)} %get-tuple-element.14.new_far, f32[640,128]{1,0:T(8,128)} %get-tuple-element.15.got_far, f32[256,128]{1,0:T(8,128)} %get-tuple-element.16.early_far, ...), custom_call_target="tpu_custom_call" | custom-call | tf_op jit(solution)/shard_map/pallas_call | solution.py:609
